TPU v7x, 256 devices: a whole 4x4x8 slice. The times are simulated.
256 devices in a mesh: freq: 4 (over z_hi, core), space: 64 (over z_lo, y, x).
Axes of the slice: x: 4, y: 4, z: 8 (z_hi: 2, z_lo: 4; z = z_hi * 4 + z_lo), core: 2. Of those that a mesh axis runs over, the one named last changes fastest.
Arguments:
- source_field: bfloat16 [2, 8, 1024, 1024], P(None, 'freq', 'space'), may hold values from -6 to 6
- receiver_field: bfloat16 [2, 8, 1024, 1024], P(None, 'freq', 'space'), may hold values from -6 to 6
- line_inverse: bfloat16 [2, 8, 1024, 1024], P(None, 'freq'), may hold values from -0.125 to 0.125
- lens_delay: float32 [3, 1024, 1024], P(None, 'space'), may hold values from -0.6 to 0.6
- omegas: float32 [8], P('freq'), may hold values from 4 to 40
- image_weights: float32 [8], P('freq'), may hold values from 0.1 to 1
Outputs:
- source_out: bfloat16 [2, 8, 1024, 1024], P(None, 'freq', 'space')
- receiver_out: bfloat16 [2, 8, 1024, 1024], P(None, 'freq', 'space')
- gradient: float32 [3, 1024, 1024], P(None, 'space')
All inputs are finite; a program needn't handle non-finite values.
Results may differ from a plain program's by a relative error of at most 0.017.
Values may be sent and summed in bfloat16 or wider, within the bound.
A program may use at most 64 MiB of HBM per device.

v0:
```python
import jax
import jax.numpy as jnp
from jax import lax
from jax.sharding import PartitionSpec as P


def to_blocks(matrix, pieces):
    leading = matrix.shape[:-2]
    local_rows = matrix.shape[-2]
    columns = matrix.shape[-1] // pieces
    arranged = matrix.reshape(leading + (local_rows, pieces, columns))
    arranged = jnp.moveaxis(arranged, -2, -3)
    return arranged.reshape(leading + (pieces, local_rows * columns))


def from_blocks(blocked, local_rows):
    leading = blocked.shape[:-2]
    pieces = blocked.shape[-2]
    columns = blocked.shape[-1] // local_rows
    arranged = blocked.reshape(leading + (pieces, local_rows, columns))
    arranged = jnp.moveaxis(arranged, -1, -3)
    return arranged.reshape(leading + (columns, pieces * local_rows))


def rotate(fields, phase_angle):
    cosine = jnp.cos(phase_angle)
    sine_part = jnp.sin(phase_angle)
    flip_sign = jnp.array([1.0, -1.0], jnp.float32).reshape(2, 1, 1, 1)
    real_part = fields[:, 0]
    imag_part = fields[:, 1]
    return jnp.stack(
        [
            real_part * cosine + flip_sign * imag_part * sine_part,
            imag_part * cosine - flip_sign * real_part * sine_part,
        ],
        axis=1,
    )


def line_solve(line_inverse, fields):
    flip_sign = jnp.array([1.0, -1.0], jnp.float32).reshape(2, 1, 1, 1)
    prod_real = jnp.einsum(
        "fij,wpfrj->wpfri", line_inverse[0], fields, preferred_element_type=jnp.float32
    )
    prod_imag = jnp.einsum(
        "fij,wpfrj->wpfri", line_inverse[1], fields, preferred_element_type=jnp.float32
    )
    new_real = prod_real[:, 0] - flip_sign * prod_imag[:, 1]
    new_imag = prod_real[:, 1] + flip_sign * prod_imag[:, 0]
    return jnp.stack([new_real, new_imag], axis=1)


def march_step(line_inverse, phased, local_rows):
    pieces = lax.axis_size("space")
    across = line_solve(line_inverse, phased).astype(jnp.bfloat16)
    received = lax.all_to_all(
        to_blocks(across, pieces), "space", split_axis=3, concat_axis=3, tiled=True
    )
    return line_solve(line_inverse, from_blocks(received, local_rows))


def image_slice(fields, image_weights):
    image_term = fields[0, 0] * fields[1, 0] + fields[0, 1] * fields[1, 1]
    return jnp.sum(image_weights[:, None, None] * image_term, axis=0)


def reduce_slice(image_term):
    return lax.psum(image_term.astype(jnp.bfloat16), "freq").astype(jnp.float32)


def finish_sums(slices):
    stacked = jnp.stack(slices)
    return stacked


def on_device(source_field, receiver_field, line_inverse, lens_delay, omegas, image_weights):
    pieces = lax.axis_size("space")
    local_rows = lens_delay.shape[1]
    depth_count = lens_delay.shape[0]
    wavefields = jnp.stack([source_field, receiver_field]).astype(jnp.float32)
    slices = []
    for depth_step in range(depth_count):
        phase_angle = omegas[:, None, None] * lens_delay[depth_step][None]
        phased = rotate(wavefields, phase_angle).astype(jnp.bfloat16)
        solved = march_step(line_inverse, phased, local_rows)
        returned = lax.all_to_all(
            to_blocks(solved, pieces), "space", split_axis=3, concat_axis=3, tiled=True
        )
        wavefields = from_blocks(returned, local_rows)
        slices.append(reduce_slice(image_slice(wavefields, image_weights)))
    gradient = finish_sums(slices)
    final_fields = wavefields.astype(jnp.bfloat16)
    return (final_fields[0], final_fields[1], gradient)


def solution(mesh):
    placed = (
        P(None, "freq", "space", None),
        P(None, "freq", "space", None),
        P(None, "freq", None, None),
        P(None, "space", None),
        P("freq"),
        P("freq"),
    )
    return jax.shard_map(
        on_device,
        mesh=mesh,
        in_specs=placed,
        out_specs=(
            P(None, "freq", "space", None),
            P(None, "freq", "space", None),
            P(None, "space", None),
        ),
        check_vma=False,
    )
```

profile of v0, /device:TPU:1, one launch (start us, length us, event | category | flops | bytes accessed | tf_op | source)
XLA Modules:
  0.0 303.4 jit_solution(14266992645873292109)
XLA Ops:
  9.3 3.0 %multiply_cosine_fusion = (f32[2,16,1024]{2,1,0:T(8,128)S(1)}, f32[2,16,1024]{2,1,0:T(8,128)}, f32[2,16,1024]{2,1,0:T(8,128)S(1)}, f32[2,16,1024]{2,1,0:T(8,128)...) fusion(f32[16,1024]{1,0:T(8,128)S(1)} %get-tuple-element.33, f32[2]{0:T(128)} %param.19, ...), kind=kLoop, calls=%fused_computation.95 | loop fusion | flops 98304 | bytes 983048 | tf_op jit(solution)/shard_map/cos | solution.py:26
  13.2 3.6 %fusion.36 = f32[2,2,2,16,1024]{4,3,1,0,2:T(8,128)S(1)} fusion(bf16[2,2,1024,1024]{3,2,1,0:T(8,128)(2,1)} %param.17, bf16[2,1,2,16,1024]{4,3,1,0,2:T(8,128)(2,1)S(1)} %get-tuple-element.26, bf16[2,1,2,16,1024]{4,3,1,0,2:T(8,128)(2,1)S(1)} %get-tuple-element.25), kind=kOutput, calls=%fused_computation.36 | convolution fusion | flops 268566528 | bytes 4980736 | tf_op jit(solution)/shard_map/fij,wpfrj->wpfri/dot_general | solution.py:45
  21.1 23.7 %all_to_all.30 = bf16[2,2,2,64,256]{4,2,1,0,3:T(2,128)(2,1)S(1)} all-to-all(bf16[2,2,2,64,256]{4,2,1,0,3:T(2,128)(2,1)S(1)} %copy.66), channel_id=1, replica_groups=mesh['freq'=4,'space'=64] {'space'}, dimensions={3} | all-to-all | bytes 524288 | tf_op jit(solution)/shard_map/all_to_all | solution.py:56
  46.2 3.6 %reshape.154 = bf16[2,2,2,16,1024]{4,3,1,0,2:T(8,128)(2,1)S(1)} reshape(bf16[2,2,2,16,64,16]{5,4,3,1,0,2:T(8,128)(2,1)S(1)} %copy.140) | data formatting | bytes 524288 | tf_op jit(solution)/shard_map/reshape | solution.py:22
  49.8 3.6 %fusion.39 = f32[2,2,2,16,1024]{4,3,1,0,2:T(8,128)S(1)} fusion(bf16[2,2,2,16,1024]{4,3,1,0,2:T(8,128)(2,1)S(1)} %reshape.154, bf16[2,2,1024,1024]{3,2,1,0:T(8,128)(2,1)} %param.17), kind=kOutput, calls=%fused_computation.37 | convolution fusion | flops 268435456 | bytes 4980736 | tf_op jit(solution)/shard_map/fij,wpfrj->wpfri/dot_general | solution.py:45
  53.4 3.6 %fusion.57 = f32[2,2,2,16,1024]{4,3,1,0,2:T(8,128)S(1)} fusion(bf16[2,2,2,16,1024]{4,3,1,0,2:T(8,128)(2,1)S(1)} %reshape.154, bf16[2,2,1024,1024]{3,2,1,0:T(8,128)(2,1)} %param.17), kind=kOutput, calls=%fused_computation.43 | convolution fusion | flops 268435456 | bytes 4980736 | tf_op jit(solution)/shard_map/fij,wpfrj->wpfri/dot_general | solution.py:42
  60.3 22.0 %all_to_all.31 = f32[2,2,2,64,256]{4,2,1,0,3:T(2,128)S(1)} all-to-all(f32[2,2,2,64,256]{4,2,1,0,3:T(2,128)S(1)} %copy.75), channel_id=1, replica_groups=mesh['freq'=4,'space'=64] {'space'}, dimensions={3} | all-to-all | bytes 1048576 | tf_op jit(solution)/shard_map/all_to_all | solution.py:86
  82.6 2.7 copy.77
  85.3 4.7 %reshape.127 = f32[2,2,2,16,1024]{4,3,2,1,0:T(8,128)S(1)} reshape(f32[2,2,2,16,64,16]{5,4,3,2,1,0:T(8,128)} %copy.77) | data formatting | bytes 1048576 | tf_op jit(solution)/shard_map/reshape | solution.py:22
  90.2 3.6 %fusion.42 = f32[2,2,2,16,1024]{4,3,1,0,2:T(8,128)S(1)} fusion(bf16[2,2,1024,1024]{3,2,1,0:T(8,128)(2,1)} %param.17, bf16[2,1,2,16,1024]{4,3,1,0,2:T(8,128)(2,1)S(1)} %get-tuple-element.24, bf16[2,1,2,16,1024]{4,3,1,0,2:T(8,128)(2,1)S(1)} %get-tuple-element.23), kind=kOutput, calls=%fused_computation.38 | convolution fusion | flops 268566528 | bytes 4980736 | tf_op jit(solution)/shard_map/fij,wpfrj->wpfri/dot_general | solution.py:45
  93.8 3.6 %fusion.60 = f32[2,2,2,16,1024]{4,3,1,0,2:T(8,128)S(1)} fusion(bf16[2,2,1024,1024]{3,2,1,0:T(8,128)(2,1)} %param.17, bf16[2,1,2,16,1024]{4,3,1,0,2:T(8,128)(2,1)S(1)} %get-tuple-element.24, bf16[2,1,2,16,1024]{4,3,1,0,2:T(8,128)(2,1)S(1)} %get-tuple-element.23), kind=kOutput, calls=%fused_computation.44 | convolution fusion | flops 268566528 | bytes 4980736 | tf_op jit(solution)/shard_map/fij,wpfrj->wpfri/dot_general | solution.py:42
  100.3 17.2 %all_to_all.32 = bf16[2,2,2,64,256]{4,2,1,0,3:T(2,128)(2,1)S(1)} all-to-all(bf16[2,2,2,64,256]{4,2,1,0,3:T(2,128)(2,1)S(1)} %copy.84), channel_id=1, replica_groups=mesh['freq'=4,'space'=64] {'space'}, dimensions={3} | all-to-all | bytes 524288 | tf_op jit(solution)/shard_map/all_to_all | solution.py:56
  118.9 3.6 %reshape.155 = bf16[2,2,2,16,1024]{4,3,1,0,2:T(8,128)(2,1)S(1)} reshape(bf16[2,2,2,16,64,16]{5,4,3,1,0,2:T(8,128)(2,1)S(1)} %copy.142) | data formatting | bytes 524288 | tf_op jit(solution)/shard_map/reshape | solution.py:22
  122.5 3.6 %fusion.45 = f32[2,2,2,16,1024]{4,3,1,0,2:T(8,128)S(1)} fusion(bf16[2,2,2,16,1024]{4,3,1,0,2:T(8,128)(2,1)S(1)} %reshape.155, bf16[2,2,1024,1024]{3,2,1,0:T(8,128)(2,1)} %param.17), kind=kOutput, calls=%fused_computation.39 | convolution fusion | flops 268435456 | bytes 4980736 | tf_op jit(solution)/shard_map/fij,wpfrj->wpfri/dot_general | solution.py:45
  126.1 3.6 %fusion.63 = f32[2,2,2,16,1024]{4,3,1,0,2:T(8,128)S(1)} fusion(bf16[2,2,2,16,1024]{4,3,1,0,2:T(8,128)(2,1)S(1)} %reshape.155, bf16[2,2,1024,1024]{3,2,1,0:T(8,128)(2,1)} %param.17), kind=kOutput, calls=%fused_computation.45 | convolution fusion | flops 268435456 | bytes 4980736 | tf_op jit(solution)/shard_map/fij,wpfrj->wpfri/dot_general | solution.py:42
  131.8 1.4 copy.92
  134.8 21.1 %all_to_all.33 = f32[2,2,2,64,256]{4,2,1,0,3:T(2,128)S(1)} all-to-all(f32[2,2,2,64,256]{4,2,1,0,3:T(2,128)S(1)} %copy.93), channel_id=1, replica_groups=mesh['freq'=4,'space'=64] {'space'}, dimensions={3} | all-to-all | bytes 1048576 | tf_op jit(solution)/shard_map/all_to_all | solution.py:86
  156.3 2.7 copy.95
  159.0 4.7 %reshape.133 = f32[2,2,2,16,1024]{4,3,2,1,0:T(8,128)S(1)} reshape(f32[2,2,2,16,64,16]{5,4,3,2,1,0:T(8,128)} %copy.95) | data formatting | bytes 1048576 | tf_op jit(solution)/shard_map/reshape | solution.py:22
  163.9 3.6 %fusion.48 = f32[2,2,2,16,1024]{4,3,1,0,2:T(8,128)S(1)} fusion(bf16[2,2,1024,1024]{3,2,1,0:T(8,128)(2,1)} %param.17, bf16[2,1,2,16,1024]{4,3,1,0,2:T(8,128)(2,1)S(1)} %get-tuple-element.22, bf16[2,1,2,16,1024]{4,3,1,0,2:T(8,128)(2,1)S(1)} %get-tuple-element.21), kind=kOutput, calls=%fused_computation.40 | convolution fusion | flops 268566528 | bytes 4980736 | tf_op jit(solution)/shard_map/fij,wpfrj->wpfri/dot_general | solution.py:45
  167.5 3.6 %fusion.66 = f32[2,2,2,16,1024]{4,3,1,0,2:T(8,128)S(1)} fusion(bf16[2,2,1024,1024]{3,2,1,0:T(8,128)(2,1)} %param.17, bf16[2,1,2,16,1024]{4,3,1,0,2:T(8,128)(2,1)S(1)} %get-tuple-element.22, bf16[2,1,2,16,1024]{4,3,1,0,2:T(8,128)(2,1)S(1)} %get-tuple-element.21), kind=kOutput, calls=%fused_computation.46 | convolution fusion | flops 268566528 | bytes 4980736 | tf_op jit(solution)/shard_map/fij,wpfrj->wpfri/dot_general | solution.py:42
  174.0 17.3 %all_to_all.34 = bf16[2,2,2,64,256]{4,2,1,0,3:T(2,128)(2,1)S(1)} all-to-all(bf16[2,2,2,64,256]{4,2,1,0,3:T(2,128)(2,1)S(1)} %copy.102), channel_id=1, replica_groups=mesh['freq'=4,'space'=64] {'space'}, dimensions={3} | all-to-all | bytes 524288 | tf_op jit(solution)/shard_map/all_to_all | solution.py:56
  192.4 1.9 copy.144
  194.3 3.6 %reshape.156 = bf16[2,2,2,16,1024]{4,3,1,0,2:T(8,128)(2,1)S(1)} reshape(bf16[2,2,2,16,64,16]{5,4,3,1,0,2:T(8,128)(2,1)S(1)} %copy.144) | data formatting | bytes 524288 | tf_op jit(solution)/shard_map/reshape | solution.py:22
  197.9 3.6 %fusion.51 = f32[2,2,2,16,1024]{4,3,1,0,2:T(8,128)S(1)} fusion(bf16[2,2,2,16,1024]{4,3,1,0,2:T(8,128)(2,1)S(1)} %reshape.156, bf16[2,2,1024,1024]{3,2,1,0:T(8,128)(2,1)} %param.17), kind=kOutput, calls=%fused_computation.41 | convolution fusion | flops 268435456 | bytes 4980736 | tf_op jit(solution)/shard_map/fij,wpfrj->wpfri/dot_general | solution.py:45
  201.5 3.6 %fusion.69 = f32[2,2,2,16,1024]{4,3,1,0,2:T(8,128)S(1)} fusion(bf16[2,2,2,16,1024]{4,3,1,0,2:T(8,128)(2,1)S(1)} %reshape.156, bf16[2,2,1024,1024]{3,2,1,0:T(8,128)(2,1)} %param.17), kind=kOutput, calls=%fused_computation.47 | convolution fusion | flops 268435456 | bytes 4980736 | tf_op jit(solution)/shard_map/fij,wpfrj->wpfri/dot_general | solution.py:42
  205.9 1.7 reshape.152
  212.8 20.0 %all_to_all.35 = f32[2,2,2,64,256]{4,2,1,0,3:T(2,128)S(1)} all-to-all(f32[2,2,2,64,256]{4,2,1,0,3:T(2,128)S(1)} %copy.111), channel_id=1, replica_groups=mesh['freq'=4,'space'=64] {'space'}, dimensions={3} | all-to-all | bytes 1048576 | tf_op jit(solution)/shard_map/all_to_all | solution.py:86
  233.2 2.7 copy.113
  235.9 4.7 %reshape.139 = f32[2,2,2,16,1024]{4,3,2,1,0:T(8,128)S(1)} reshape(f32[2,2,2,16,64,16]{5,4,3,2,1,0:T(8,128)} %copy.113) | data formatting | bytes 1048576 | tf_op jit(solution)/shard_map/reshape | solution.py:22
  242.1 52.8 %all-reduce.3.cloned.1.call-done = (bf16[1,16,1024]{2,1,0:T(8,128)(2,1)}, bf16[1,16,1024]{2,1,0:T(8,128)(2,1)}, bf16[1,16,1024]{2,1,0:T(8,128)(2,1)}) async-done(((bf16[1,16,1024]{2,1,0:T(8,128)(2,1)}, bf16[1,16,1024]{2,1,0:T(8,128)(2,1)}, bf16[1,16,1024]{2,1,0:T(8,128)(2,1)}), (bf16[1,16,1024]{2,1,0:T(8,128)(2,1)}, bf16[1,16,1024]{2,1,0:T(8,128)(2,1)}, ...) | async-done | bytes 98320 | tf_op jit(solution)/shard_map/psum | solution.py:68
  294.9 1.5 maximum_convert_fusion.1
  (70 shorter events, 32.9 us)
Async XLA Ops:
  7.2 287.7 %all-reduce.3.cloned.1.call-start = ((), (), s32[]{:S(2)}) async-start(), calls=%async_computation.6 | async-start | bytes 196608 | tf_op jit(solution)/shard_map/psum | solution.py:68
  8.1 8.7 %copy-start.3 = (bf16[2,2,1024,1024]{3,2,1,0:T(8,128)(2,1)S(1)}, bf16[2,2,1024,1024]{3,2,1,0:T(8,128)(2,1)}, u32[]{:S(2)}) copy-start(bf16[2,2,1024,1024]{3,2,1,0:T(8,128)(2,1)} %param.17) | copy-start | bytes 25165828
  13.2 5.0 %copy-start.1 = (f32[2]{0:T(128)S(1)}, f32[2]{0:T(128)}, u32[]{:S(2)}) copy-start(f32[2]{0:T(128)} %constant.4.clone) | copy-start | bytes 28
  159.0 4.8 %copy-start = (f32[2,16,1024]{2,1,0:T(8,128)S(1)}, f32[2,16,1024]{2,1,0:T(8,128)}, u32[]{:S(2)}) copy-start(f32[2,16,1024]{2,1,0:T(8,128)} %get-tuple-element.37) | copy-start | bytes 393220
  233.2 7.4 %copy-start.2 = (f32[2]{0:T(128)S(1)}, f32[2]{0:T(128)}, u32[]{:S(2)}) copy-start(f32[2]{0:T(128)} %param.20) | copy-start | bytes 28
Sparse Core Ops, SparseCore 0:
  241.5 53.3 all-reduce.2
where the time goes:
time: 309 us; the launch traced here: 303 us
  blocking collectives  121 us (39%)
  local copies, waits for them, and re-layouts  63.1 us (20%)
  waiting for transfers between devices  52.8 us (17%)
  matrix products  40.8 us (13%)
  between operations  14.7 us (5%)
  other arithmetic  10.8 us (3%)
    all_to_all x3, blocking collectives, on_device(): lax.all_to_all(to_blocks(solved, pieces), 'space', split_axis=3, concat_a...  63.1 us
    all_to_all x3, blocking collectives, march_step(): lax.all_to_all(to_blocks(across, pieces), 'space', split_axis=3, concat_a...  58.2 us
    psum x1, waiting for transfers between devices, reduce_slice(): return lax.psum(image_term.astype(jnp.bfloat16), 'freq').astype(jnp.float32)  52.8 us
    reshape x9, local copies, waits for them, and re-layouts, from_blocks(): return arranged.reshape(leading + (columns, pieces * local_rows))  28.9 us
    dot_general x6, matrix products, line_solve(): jnp.einsum('fij,wpfrj->wpfri', line_inverse[1], fields, preferred_element...  21.5 us
    dot_general x6, matrix products, line_solve(): jnp.einsum('fij,wpfrj->wpfri', line_inverse[0], fields, preferred_element...  19.3 us
    another operation x24, local copies, waits for them, and re-layouts, line_solve(): return jnp.stack([new_real, new_imag], axis=1)  18.3 us
    transpose x3, local copies, waits for them, and re-layouts, from_blocks(): arranged = jnp.moveaxis(arranged, -1, -3)  8.01 us
  transfers between devices with their start and end apart: 1, of which 1 were waited for; matrix products, arithmetic and copies ran while one was open for 0% of the time, Pallas kernels for 0%

commit v1 on v0

v1 whole, which is shorter than its diff:
```python
import jax
import jax.numpy as jnp
from jax import lax
from jax.experimental import pallas as pl
from jax.experimental.pallas import tpu as pltpu
from jax.sharding import PartitionSpec as P

F32 = jnp.float32
BF16 = jnp.bfloat16
MESH = pl.DeviceIdType.MESH
LANES = 128
BLOCK = 32
NL = 1024
ROWS = 16
GROUP = 32
SHARDS = 64
CHUNK = 256
NT = (((1,), (1,)), ((), ()))
SWAP_SIGN = (-1.0, 1.0, 1.0, -1.0)

(A2A1, A2A2, A2A3, A2A4, LENS1, LENS2, FWD1, FWD2,
 SUM0, DIST0, SUM1, DIST1, PAIR, CROSS) = range(14)
PHASES = 14


def lanes(tile):
    return lax.broadcasted_iota(jnp.int32, tile.shape, 1)


def turn(tile, shift):
    return pltpu.roll(tile, shift % LANES, 1)


def even_block(tile):
    return (lanes(tile) // BLOCK) % 2 == 0


def block_transpose(tiles):
    t0, t1, t2, t3 = tiles
    low = lanes(t0) < 64
    even = even_block(t0)
    a0, a2 = jnp.where(low, t0, turn(t2, 64)), jnp.where(low, turn(t0, 64), t2)
    a1, a3 = jnp.where(low, t1, turn(t3, 64)), jnp.where(low, turn(t1, 64), t3)
    b0, b1 = jnp.where(even, a0, turn(a1, 32)), jnp.where(even, turn(a0, -32), a1)
    b2, b3 = jnp.where(even, a2, turn(a3, 32)), jnp.where(even, turn(a2, -32), a3)
    return b0, b1, b2, b3


def swap_parts(tile):
    return jnp.where(even_block(tile), turn(tile, -32), turn(tile, 32))


def outer_sign(tile):
    block = lanes(tile) // BLOCK
    return jnp.where((block == 0) | (block == 3), -1.0, 1.0)


def cos_sin(theta):
    n = jnp.floor(theta * 0.3183098861837907 + 0.5)
    r = theta - n * 3.140625
    r = r - n * 9.67502593994140625e-4
    r = r - n * 1.509957990978376e-7
    flip = 1.0 - 2.0 * (n - 2.0 * jnp.floor(n * 0.5))
    z = r * r
    s = -1.0 / 39916800.0
    for term in (1.0 / 362880.0, -1.0 / 5040.0, 1.0 / 120.0, -1.0 / 6.0, 1.0):
        s = s * z + term
    c = 1.0 / 479001600.0
    for term in (-1.0 / 3628800.0, 1.0 / 40320.0, -1.0 / 720.0, 1.0 / 24.0, -0.5, 1.0):
        c = c * z + term
    return c * flip, s * r * flip


def at(index, size):
    return pl.ds(pl.multiple_of(index * size, size), size)


def kernel(src, rcv, minv, lens, om, wt, src_out, rcv_out, grad,
           src_v, rcv_v, lens_v, m, send1, got1, send2, got2, send3, got3, send4, got4,
           ya, yb, xa, xb, xf, cos1, sin1, cos2, sin2, lens1, lens2_send, lens2,
           part0, sum0, dist0_send, dist0, part1, sum1, dist1_send, dist1,
           pair, cross, load_sem, ss, rs):
    fq = lax.axis_index("freq")
    s = lax.axis_index("space")
    h = s // GROUP
    k = lax.rem(s, GROUP)
    core = lax.rem(fq, 2)
    z_hi = fq // 2
    rank = 2 * fq + h
    mine = lax.rem(s, 2) == core
    om_h = om[h]
    wt_h = wt[h]

    def remote(source, target, phase, freq, space):
        return pltpu.make_async_remote_copy(
            src_ref=source, dst_ref=target, send_sem=ss.at[phase], recv_sem=rs.at[phase],
            device_id={"freq": freq, "space": space}, device_id_type=MESH)

    def wait_on(sem, ref):
        pltpu.make_async_copy(ref, ref, sem).wait()

    def give(source, target, phase, freq, space):
        here = (freq == fq) & (space == s)

        @pl.when(here)
        def _():
            pltpu.make_async_copy(source, target, rs.at[phase]).start()

        @pl.when(jnp.logical_not(here))
        def _():
            remote(source, target, phase, freq, space).start()

    loads = [
        pltpu.make_async_copy(src, src_v, load_sem.at[0]),
        pltpu.make_async_copy(rcv, rcv_v, load_sem.at[1]),
        pltpu.make_async_copy(lens, lens_v, load_sem.at[2]),
        pltpu.make_async_copy(minv.at[:, h], m.at[0], load_sem.at[3]),
        pltpu.make_async_copy(minv.at[:, 1 - h], m.at[1], load_sem.at[4]),
    ]
    for load in loads:
        load.start()
    barrier = pltpu.get_barrier_semaphore()

    def greet(i, carry):
        pl.semaphore_signal(barrier, inc=1, device_id={"freq": fq, "space": lax.rem(s + i, SHARDS)},
                            device_id_type=MESH)
        return carry

    lax.fori_loop(1, SHARDS, greet, 0)
    for i in range(1, 4):
        pl.semaphore_signal(barrier, inc=1, device_id={"freq": lax.rem(fq + i, 4), "space": s},
                            device_id_type=MESH)
    for load in loads[:3]:
        load.wait()

    def rotate0(i, carry):
        f = i // 8
        q = lax.rem(i, 8)
        c, sn = cos_sin(om[f] * lens_v[0, :, at(q, LANES)])
        sre = src_v[0, f, :, at(q, LANES)].astype(F32)
        sim = src_v[1, f, :, at(q, LANES)].astype(F32)
        rre = rcv_v[0, f, :, at(q, LANES)].astype(F32)
        rim = rcv_v[1, f, :, at(q, LANES)].astype(F32)
        tiles = block_transpose((sre * c + sim * sn, sim * c - sre * sn,
                                 rre * c - rim * sn, rim * c + rre * sn))
        for p in range(4):
            send1[at(f * GROUP + 4 * q + p, ROWS), :] = tiles[p].astype(BF16)
        return carry

    lax.fori_loop(0, 16, rotate0, 0)
    got1[at(s, ROWS), :] = send1[at(s, ROWS), :]
    pl.semaphore_wait(barrier, SHARDS - 1 + 3)

    def go1(i, carry):
        t = lax.rem(s + i, SHARDS)
        remote(send1.at[at(t, ROWS)], got1.at[at(s, ROWS)], A2A1, fq, t).start()
        return carry

    lax.fori_loop(1, SHARDS, go1, 0)

    @pl.when(mine)
    def _():
        for half in range(2):
            give(lens_v.at[1], lens1.at[core], LENS1, fq, half * GROUP + s // 2)

    def pack2(q, carry):
        value = lens_v[2, :, at(q, LANES)]
        high = value.astype(BF16).astype(F32)
        rest = value - high
        middle = rest.astype(BF16).astype(F32)
        tiles = block_transpose((high, middle, rest - middle, jnp.zeros_like(value)))
        for p in range(4):
            lens2_send[at(4 * q + p, ROWS), :] = tiles[p].astype(BF16)
        return carry

    lax.fori_loop(0, 8, pack2, 0)

    def y_operands(got, other):
        def body(i, carry):
            tile = got[at(i, 128), :].astype(F32)
            other[at(i, 128), :] = (swap_parts(tile) * outer_sign(tile)).astype(BF16)
            return carry

        lax.fori_loop(0, 8, body, 0)

    def y_solve(first, second, n):
        rows = at(n, CHUNK)
        return (jnp.dot(m[0, 0, rows, :], first[...], preferred_element_type=F32)
                + jnp.dot(m[0, 1, rows, :], second[...], preferred_element_type=F32))

    def x_solve(f, first, second, n):
        rows = at(n, CHUNK)
        return (lax.dot_general(first, m[f, 0, rows, :], NT, preferred_element_type=F32)
                + lax.dot_general(second, m[f, 1, rows, :], NT, preferred_element_type=F32))

    def send_group(send, got, phase, n):
        def body(i, carry):
            t = n * 8 + lax.rem(k + i, 8)

            @pl.when(t != k)
            def _():
                remote(send.at[at(t, BLOCK)], got.at[at(k, BLOCK)], phase, fq, h * GROUP + t).start()

            return carry

        lax.fori_loop(0, 8, body, 0)

    loads[3].wait()
    wait_on(rs.at[A2A1], got1.at[pl.ds(0, ROWS * (SHARDS - 1))])
    y_operands(got1, ya)

    def solve1(i, carry):
        n = lax.rem(k // 8 + i, 4)
        send2[at(n, CHUNK), :] = y_solve(got1, ya, n).astype(BF16)
        send_group(send2, got2, A2A2, n)
        return carry

    lax.fori_loop(0, 4, solve1, 0)
    got2[at(k, BLOCK), :] = send2[at(k, BLOCK), :]

    wait_on(rs.at[LENS1], lens1.at[0])
    forward1 = remote(lens1.at[core], lens1.at[core], FWD1, fq + 1 - 2 * core, s)
    forward1.start()

    skew = jnp.where(mine, 0, 1)

    def go_lens2(i, carry):
        t = lax.rem(s + skew + 2 * i, SHARDS)

        @pl.when(t != s)
        def _():
            remote(lens2_send.at[at(lax.rem(t, GROUP), ROWS)], lens2.at[at(s, ROWS)], LENS2, fq, t).start()

        return carry

    lax.fori_loop(0, 32, go_lens2, 0)

    @pl.when(mine)
    def _():
        lens2[at(s, ROWS), :] = lens2_send[at(k, ROWS), :]

    forward1.wait_recv()

    def trig1(q, carry):
        for b in range(2):
            c, sn = cos_sin(om_h * lens1[b, :, at(q, LANES)])
            cos1[pl.ds(b * ROWS, ROWS), at(q, LANES)] = c
            sin1[pl.ds(b * ROWS, ROWS), at(q, LANES)] = sn
        return carry

    lax.fori_loop(0, 8, trig1, 0)

    wait_on(rs.at[A2A2], got2.at[pl.ds(0, BLOCK * (GROUP - 1))])

    def gather2(q, carry):
        tiles = block_transpose([got2[at(4 * q + p, BLOCK), :].astype(F32) for p in range(4)])
        for c in range(4):
            xa[0, pl.ds(c * BLOCK, BLOCK), at(q, LANES)] = tiles[c].astype(BF16)
            xa[1, pl.ds(c * BLOCK, BLOCK), at(q, LANES)] = (SWAP_SIGN[c] * tiles[c ^ 1]).astype(BF16)
        return carry

    lax.fori_loop(0, 8, gather2, 0)

    def solve2(n, carry):
        new = x_solve(0, xa[0], xa[1], n)
        sre, sim, rre, rim = (new[c * BLOCK:(c + 1) * BLOCK] for c in range(4))
        image = wt_h * (sre * rre + sim * rim)
        for u in range(2):
            part0[2 * n + u] = image[:, u * LANES:(u + 1) * LANES].astype(BF16)
        c, sn = cos1[:, at(n, CHUNK)], sin1[:, at(n, CHUNK)]
        turned = (sre * c + sim * sn, sim * c - sre * sn, rre * c - rim * sn, rim * c + rre * sn)
        for part in range(4):
            xb[0, pl.ds(part * BLOCK, BLOCK), at(n, CHUNK)] = turned[part].astype(BF16)
            xb[1, pl.ds(part * BLOCK, BLOCK), at(n, CHUNK)] = (
                SWAP_SIGN[part] * turned[part ^ 1]).astype(BF16)
        return carry

    lax.fori_loop(0, 4, solve2, 0)

    def solve3(i, carry):
        n = lax.rem(k // 8 + i, 4)
        new = x_solve(0, xb[0], xb[1], n)
        for u in range(2):
            tiles = block_transpose([new[c * BLOCK:(c + 1) * BLOCK, u * LANES:(u + 1) * LANES]
                                     for c in range(4)])
            for p in range(4):
                send3[at(8 * n + 4 * u + p, BLOCK), :] = tiles[p].astype(BF16)
        send_group(send3, got3, A2A3, n)
        return carry

    lax.fori_loop(0, 4, solve3, 0)
    got3[at(k, BLOCK), :] = send3[at(k, BLOCK), :]

    def sum_send(part, total, phase):
        total[rank] = part[rank]

        def body(i, carry):
            j = lax.rem(rank + i, 8)
            remote(part.at[j], total.at[rank], phase, j // 2, lax.rem(j, 2) * GROUP + k).start()
            return carry

        lax.fori_loop(1, 8, body, 0)

    def sum_up(total, phase):
        wait_on(rs.at[phase], total.at[pl.ds(0, 7)])
        value = total[0].astype(F32)
        for j in range(1, 8):
            value += total[j].astype(F32)
        return value

    sum_send(part0, sum0, SUM0)

    forward2 = remote(lens2, lens2, FWD2, fq + 1 - 2 * core, s)

    @pl.when(mine)
    def _():
        wait_on(rs.at[LENS2], lens2.at[pl.ds(0, ROWS * (SHARDS - 1))])
        forward2.start()

    @pl.when(jnp.logical_not(mine))
    def _():
        forward2.wait_recv()

    def trig2(i, carry):
        terms = lens2[at(i, 128), :].astype(F32)
        value = (terms + turn(terms, -32)) + turn(terms, -64)
        value = jnp.where(lanes(value) < BLOCK, value, 0.0)
        value = value + turn(value, 32)
        value = value + turn(value, 64)
        c, sn = cos_sin(om_h * value)
        cos2[at(i, 128), :] = c
        sin2[at(i, 128), :] = -outer_sign(sn) * sn
        return carry

    lax.fori_loop(0, 8, trig2, 0)

    dist0_send[...] = sum_up(sum0, SUM0).astype(BF16)
    for f in range(4):
        for b in range(2):
            give(dist0_send.at[pl.ds(b * ROWS, ROWS)], dist0.at[rank], DIST0, f, 2 * k + b)

    wait_on(rs.at[A2A3], got3.at[pl.ds(0, BLOCK * (GROUP - 1))])
    y_operands(got3, ya)

    def solve4(n, carry):
        new = y_solve(got3, ya, n)
        product = wt_h * new * turn(new, 64)
        image = product + turn(product, -32)
        for u in range(2):
            packed = image[u * 128:u * 128 + BLOCK]
            block = lanes(packed) // BLOCK
            for a in range(1, 4):
                rows = image[u * 128 + a * BLOCK:u * 128 + (a + 1) * BLOCK]
                packed = jnp.where(block == a, turn(rows, a * BLOCK), packed)
            part1[2 * n + u] = packed.astype(BF16)
        turned = new * cos2[at(n, CHUNK), :] + swap_parts(new) * sin2[at(n, CHUNK), :]
        yb[0, at(n, CHUNK), :] = turned.astype(BF16)
        yb[1, at(n, CHUNK), :] = (swap_parts(turned) * outer_sign(turned)).astype(BF16)
        return carry

    lax.fori_loop(0, 4, solve4, 0)
    sum_send(part1, sum1, SUM1)

    def solve5(i, carry):
        n = lax.rem(s // 16 + i, 4)
        send4[at(n, CHUNK), :] = y_solve(yb.at[0], yb.at[1], n).astype(BF16)

        def body(j, inner):
            t = n * 16 + lax.rem(s + j, 16)

            @pl.when(t != s)
            def _():
                remote(send4.at[at(t, ROWS)], got4.at[at(s, ROWS)], A2A4, fq, t).start()

            return inner

        lax.fori_loop(0, 16, body, 0)
        return carry

    lax.fori_loop(0, 4, solve5, 0)
    got4[at(s, ROWS), :] = send4[at(s, ROWS), :]

    total1 = sum_up(sum1, SUM1)
    for d in range(4):
        dist1_send[d] = turn(total1, d * BLOCK).astype(BF16)

    def go_dist1(i, carry):
        f = i // 8
        a = lax.rem(i, 8) // 2
        b = lax.rem(i, 2)
        d = lax.rem(k + 4 - a, 4)
        give(dist1_send.at[d, at(b, ROWS)], dist1.at[k], DIST1, f, 8 * rank + lax.rem(i, 8))
        return carry

    lax.fori_loop(0, 32, go_dist1, 0)

    loads[4].wait()
    wait_on(rs.at[A2A4], got4.at[pl.ds(0, ROWS * (SHARDS - 1))])

    def gather4(i, carry):
        f = i // 8
        q = lax.rem(i, 8)
        tiles = block_transpose([got4[at(f * GROUP + 4 * q + p, ROWS), :].astype(F32) for p in range(4)])
        for c in range(4):
            xf[f, 0, pl.ds(c * ROWS, ROWS), at(q, LANES)] = tiles[c].astype(BF16)
            xf[f, 1, pl.ds(c * ROWS, ROWS), at(q, LANES)] = (SWAP_SIGN[c] * tiles[c ^ 1]).astype(BF16)
        return carry

    lax.fori_loop(0, 16, gather4, 0)

    def solve6(n, carry):
        image = jnp.zeros((ROWS, CHUNK), F32)
        for f in range(2):
            which = jnp.where(h == f, 0, 1)
            new = x_solve(which, xf[f, 0], xf[f, 1], n)
            sre, sim, rre, rim = (new[c * ROWS:(c + 1) * ROWS] for c in range(4))
            src_out[0, f, :, at(n, CHUNK)] = sre.astype(BF16)
            src_out[1, f, :, at(n, CHUNK)] = sim.astype(BF16)
            rcv_out[0, f, :, at(n, CHUNK)] = rre.astype(BF16)
            rcv_out[1, f, :, at(n, CHUNK)] = rim.astype(BF16)
            image += wt[f] * (sre * rre + sim * rim)
        pair[core, :, at(n, CHUNK)] = image.astype(BF16)
        return carry

    lax.fori_loop(0, 4, solve6, 0)
    to_pair = remote(pair.at[core], pair.at[core], PAIR, fq + 1 - 2 * core, s)
    to_pair.start()

    wait_on(rs.at[DIST0], dist0)
    wait_on(rs.at[DIST1], dist1)
    for j in range(8):
        grad[0, :, pl.ds(j * LANES, LANES)] = dist0[j].astype(F32)
        tile = dist1[4 * j].astype(F32)
        block = lanes(tile) // BLOCK
        for p in range(1, 4):
            tile = jnp.where(block == p, dist1[4 * j + p].astype(F32), tile)
        grad[1, :, pl.ds(j * LANES, LANES)] = tile

    to_pair.wait_recv()
    cross[z_hi] = (pair[0].astype(F32) + pair[1].astype(F32)).astype(BF16)
    to_cross = remote(cross.at[z_hi], cross.at[z_hi], CROSS, lax.rem(fq + 2, 4), s)
    to_cross.start()

    wait_on(ss.at[A2A1], send1.at[pl.ds(0, ROWS * (SHARDS - 1))])
    wait_on(ss.at[A2A2], send2.at[pl.ds(0, BLOCK * (GROUP - 1))])
    wait_on(ss.at[A2A3], send3.at[pl.ds(0, BLOCK * (GROUP - 1))])
    wait_on(ss.at[A2A4], send4.at[pl.ds(0, ROWS * (SHARDS - 1))])
    wait_on(ss.at[SUM0], part0.at[pl.ds(0, 7)])
    wait_on(ss.at[SUM1], part1.at[pl.ds(0, 7)])
    forward1.wait_send()

    own1 = (s == 0) | (s == SHARDS - 1)

    @pl.when(mine & own1)
    def _():
        wait_on(ss.at[LENS1], lens_v.at[1])

    @pl.when(mine & jnp.logical_not(own1))
    def _():
        wait_on(ss.at[LENS1], lens_v.at[pl.ds(0, 2)])

    @pl.when(mine)
    def _():
        wait_on(ss.at[LENS2], lens2_send.at[pl.ds(0, ROWS * 31)])
        forward2.wait_send()

    @pl.when(jnp.logical_not(mine))
    def _():
        wait_on(ss.at[LENS2], lens2_send)

    @pl.when(own1)
    def _():
        wait_on(ss.at[DIST0], dist0.at[pl.ds(0, 7)])

    @pl.when(jnp.logical_not(own1))
    def _():
        wait_on(ss.at[DIST0], dist0)

    own_dist = s // 8 == rank

    @pl.when(own_dist)
    def _():
        wait_on(ss.at[DIST1], dist1.at[pl.ds(0, 31)])

    @pl.when(jnp.logical_not(own_dist))
    def _():
        wait_on(ss.at[DIST1], dist1)

    to_pair.wait_send()
    to_cross.wait()
    grad[2] = cross[0].astype(F32) + cross[1].astype(F32)


def on_device(source_field, receiver_field, line_inverse, lens_delay, omegas, image_weights):
    vmem = pltpu.VMEM
    plane = vmem((NL, LANES), BF16)
    return pl.pallas_call(
        kernel,
        out_shape=(
            jax.ShapeDtypeStruct(source_field.shape, BF16),
            jax.ShapeDtypeStruct(receiver_field.shape, BF16),
            jax.ShapeDtypeStruct(lens_delay.shape, F32),
        ),
        in_specs=[pl.BlockSpec(memory_space=pl.ANY)] * 4 + [pl.BlockSpec(memory_space=pltpu.SMEM)] * 2,
        out_specs=[pl.BlockSpec(memory_space=vmem)] * 3,
        scratch_shapes=[
            vmem(source_field.shape, BF16), vmem(receiver_field.shape, BF16), vmem(lens_delay.shape, F32),
            vmem((2, 2, NL, NL), BF16),
            plane, plane, plane, plane, plane, plane, plane, plane,
            plane, vmem((2, NL, LANES), BF16),
            vmem((2, LANES, NL), BF16), vmem((2, LANES, NL), BF16), vmem((2, 2, 64, NL), BF16),
            vmem((BLOCK, NL), F32), vmem((BLOCK, NL), F32),
            vmem((NL, LANES), F32), vmem((NL, LANES), F32),
            vmem((2, ROWS, NL), F32), vmem((GROUP * ROWS, LANES), BF16), plane,
            vmem((8, BLOCK, LANES), BF16), vmem((8, BLOCK, LANES), BF16),
            vmem((BLOCK, LANES), BF16), vmem((8, ROWS, LANES), BF16),
            vmem((8, BLOCK, LANES), BF16), vmem((8, BLOCK, LANES), BF16),
            vmem((4, BLOCK, LANES), BF16), vmem((GROUP, ROWS, LANES), BF16),
            vmem((2, ROWS, NL), BF16), vmem((2, ROWS, NL), BF16),
            pltpu.SemaphoreType.DMA((5,)),
            pltpu.SemaphoreType.DMA((PHASES,)),
            pltpu.SemaphoreType.DMA((PHASES,)),
        ],
        compiler_params=pltpu.CompilerParams(
            collective_id=0, has_side_effects=True, vmem_limit_bytes=40 * 2**20),
    )(source_field, receiver_field, line_inverse, lens_delay, omegas, image_weights)


def solution(mesh):
    placed = (
        P(None, "freq", "space", None),
        P(None, "freq", "space", None),
        P(None, "freq", None, None),
        P(None, "space", None),
        P("freq"),
        P("freq"),
    )
    return jax.shard_map(
        on_device,
        mesh=mesh,
        in_specs=placed,
        out_specs=(
            P(None, "freq", "space", None),
            P(None, "freq", "space", None),
            P(None, "space", None),
        ),
        check_vma=False,
    )
```

time: 309 us -> 80.7 us (0.26)
  the two profiles are of different devices: /device:TPU:1 before, /device:TPU:33 now
where the time goes in v1:
time: 80.7 us; the launch traced here: 80.5 us
  Pallas kernels  70.5 us (87%)
  local copies, waits for them, and re-layouts  9.41 us (12%)
    pallas_call x1, Pallas kernels, on_device(): pl.pallas_call(kernel, out_shape=(jax.ShapeDtypeStruct(source_field.shape...  70.5 us
    unnamed x15, local copies, waits for them, and re-layouts  9.41 us

profile of v1, /device:TPU:33, one launch (start us, length us, event | category | flops | bytes accessed | tf_op | source)
XLA Modules:
  0.0 80.5 jit_solution(4403417278842178674)
XLA Ops:
  0.6 0.0 copy-start
  0.6 3.4 %copy-done = bf16[2,2,1024,1024]{3,2,1,0:T(8,128)(2,1)S(1)} copy-done((bf16[2,2,1024,1024]{3,2,1,0:T(8,128)(2,1)S(1)}, bf16[2,2,1024,1024]{3,2,1,0:T(8,128)(2,1)}, u32[]{:S(2)}) %copy-start) | copy-done | bytes 8388632
  4.0 0.0 copy-start.1
  4.0 0.9 %copy-done.1 = f32[3,16,1024]{2,1,0:T(8,128)S(1)} copy-done((f32[3,16,1024]{2,1,0:T(8,128)S(1)}, f32[3,16,1024]{2,1,0:T(8,128)}, u32[]{:S(2)}) %copy-start.1) | copy-done | bytes 196632
  4.9 0.0 copy-start.2
  4.9 0.9 %copy-done.2 = bf16[2,2,16,1024]{3,2,1,0:T(8,128)(2,1)S(1)} copy-done((bf16[2,2,16,1024]{3,2,1,0:T(8,128)(2,1)S(1)}, bf16[2,2,16,1024]{3,2,1,0:T(8,128)(2,1)}, u32[]{:S(2)}) %copy-start.2) | copy-done | bytes 131096
  5.8 0.0 copy-start.3
  5.8 0.9 %copy-done.3 = bf16[2,2,16,1024]{3,2,1,0:T(8,128)(2,1)S(1)} copy-done((bf16[2,2,16,1024]{3,2,1,0:T(8,128)(2,1)S(1)}, bf16[2,2,16,1024]{3,2,1,0:T(8,128)(2,1)}, u32[]{:S(2)}) %copy-start.3) | copy-done | bytes 131096
  6.8 0.0 copy-start.4
  6.8 0.7 copy-done.4
  7.4 0.0 copy-start.5
  7.4 0.7 copy-done.5
  8.1 70.5 %shard_map.85 = (bf16[2,2,16,1024]{3,2,1,0:T(8,128)(2,1)S(1)}, bf16[2,2,16,1024]{3,2,1,0:T(8,128)(2,1)S(1)}, f32[3,16,1024]{2,1,0:T(8,128)S(1)}) custom-call(bf16[2,2,16,1024]{3,2,1,0:T(8,128)(2,1)S(1)} %copy-done.2, bf16[2,2,16,1024]{3,2,1,0:T(8,128)(2,1)S(1)} %copy-done.3, bf16[2,2,1024,1024]{3,2,1,0:T(8,128)(2,1)S(1)} %copy-done, ...), custom_call_target="tpu_custom_call" | custom-call | tf_op jit(solution)/shard_map/pallas_call | solution.py:497
  78.5 0.7 copy.12
  79.2 0.7 copy.13
  79.9 0.7 copy.14
Async XLA Ops:
  0.6 3.4 %copy-start = (bf16[2,2,1024,1024]{3,2,1,0:T(8,128)(2,1)S(1)}, bf16[2,2,1024,1024]{3,2,1,0:T(8,128)(2,1)}, u32[]{:S(2)}) copy-start(bf16[2,2,1024,1024]{3,2,1,0:T(8,128)(2,1)} %minv.1) | copy-start | bytes 25165828
  4.0 0.9 %copy-start.1 = (f32[3,16,1024]{2,1,0:T(8,128)S(1)}, f32[3,16,1024]{2,1,0:T(8,128)}, u32[]{:S(2)}) copy-start(f32[3,16,1024]{2,1,0:T(8,128)} %lens.1) | copy-start | bytes 589828
  4.9 0.9 %copy-start.2 = (bf16[2,2,16,1024]{3,2,1,0:T(8,128)(2,1)S(1)}, bf16[2,2,16,1024]{3,2,1,0:T(8,128)(2,1)}, u32[]{:S(2)}) copy-start(bf16[2,2,16,1024]{3,2,1,0:T(8,128)(2,1)} %src.1) | copy-start | bytes 393220
  5.8 0.9 %copy-start.3 = (bf16[2,2,16,1024]{3,2,1,0:T(8,128)(2,1)S(1)}, bf16[2,2,16,1024]{3,2,1,0:T(8,128)(2,1)}, u32[]{:S(2)}) copy-start(bf16[2,2,16,1024]{3,2,1,0:T(8,128)(2,1)} %rcv.1) | copy-start | bytes 393220
  6.8 0.7 copy-start.4
  7.4 0.7 copy-start.5

commit v2 on v1

--- a/solution.py
+++ b/solution.py
@@ -15,12 +15,11 @@
 GROUP = 32
 SHARDS = 64
 CHUNK = 256
-NT = (((1,), (1,)), ((), ()))
 SWAP_SIGN = (-1.0, 1.0, 1.0, -1.0)
 
 (A2A1, A2A2, A2A3, A2A4, LENS1, LENS2, FWD1, FWD2,
- SUM0, DIST0, SUM1, DIST1, PAIR, CROSS) = range(14)
-PHASES = 14
+ SUM0, DIST0, SUM1, DIST1, PAIR, _, _, _, CROSS, _, _, _) = range(20)
+PHASES = 20
 
 
 def lanes(tile):
@@ -72,14 +71,15 @@
 
 
 def at(index, size):
-    return pl.ds(pl.multiple_of(index * size, size), size)
-
-
-def kernel(src, rcv, minv, lens, om, wt, src_out, rcv_out, grad,
-           src_v, rcv_v, lens_v, m, send1, got1, send2, got2, send3, got3, send4, got4,
+    start = index * size
+    return pl.ds(start if isinstance(start, int) else pl.multiple_of(start, size), size)
+
+
+def kernel(src, rcv, minv, lens, om_hbm, wt_hbm, src_out, rcv_out, grad,
+           src_v, rcv_v, lens_v, m, mt, send1, got1, send2, got2, send3, got3, send4, got4,
            ya, yb, xa, xb, xf, cos1, sin1, cos2, sin2, lens1, lens2_send, lens2,
            part0, sum0, dist0_send, dist0, part1, sum1, dist1_send, dist1,
-           pair, cross, load_sem, ss, rs):
+           pair, cross, om, wt, load_sem, ss, rs):
     fq = lax.axis_index("freq")
     s = lax.axis_index("space")
     h = s // GROUP
@@ -88,8 +88,6 @@
     z_hi = fq // 2
     rank = 2 * fq + h
     mine = lax.rem(s, 2) == core
-    om_h = om[h]
-    wt_h = wt[h]
 
     def remote(source, target, phase, freq, space):
         return pltpu.make_async_remote_copy(
@@ -114,12 +112,26 @@
         pltpu.make_async_copy(src, src_v, load_sem.at[0]),
         pltpu.make_async_copy(rcv, rcv_v, load_sem.at[1]),
         pltpu.make_async_copy(lens, lens_v, load_sem.at[2]),
+        pltpu.make_async_copy(om_hbm, om, load_sem.at[5]),
+        pltpu.make_async_copy(wt_hbm, wt, load_sem.at[6]),
         pltpu.make_async_copy(minv.at[:, h], m.at[0], load_sem.at[3]),
         pltpu.make_async_copy(minv.at[:, 1 - h], m.at[1], load_sem.at[4]),
     ]
     for load in loads:
         load.start()
     barrier = pltpu.get_barrier_semaphore()
+    pending = []
+    own1 = (s == 0) | (s == SHARDS - 1)
+
+    def sent(phase, ref, condition=None):
+        def wait():
+            if condition is None:
+                wait_on(ss.at[phase], ref)
+            else:
+                pl.when(condition)(lambda: wait_on(ss.at[phase], ref))
+
+        pending.append(wait)
+
 
     def greet(i, carry):
         pl.semaphore_signal(barrier, inc=1, device_id={"freq": fq, "space": lax.rem(s + i, SHARDS)},
@@ -130,8 +142,10 @@
     for i in range(1, 4):
         pl.semaphore_signal(barrier, inc=1, device_id={"freq": lax.rem(fq + i, 4), "space": s},
                             device_id_type=MESH)
-    for load in loads[:3]:
+    for load in loads[:5]:
         load.wait()
+    om_h = om[h]
+    wt_h = wt[h]
 
     def rotate0(i, carry):
         f = i // 8
@@ -157,11 +171,15 @@
         return carry
 
     lax.fori_loop(1, SHARDS, go1, 0)
+    sent(A2A1, send1.at[pl.ds(0, ROWS * (SHARDS - 1))])
 
     @pl.when(mine)
     def _():
         for half in range(2):
             give(lens_v.at[1], lens1.at[core], LENS1, fq, half * GROUP + s // 2)
+
+    sent(LENS1, lens_v.at[1], mine & own1)
+    sent(LENS1, lens_v.at[pl.ds(0, 2)], mine & jnp.logical_not(own1))
 
     def pack2(q, carry):
         value = lens_v[2, :, at(q, LANES)]
@@ -189,9 +207,18 @@
                 + jnp.dot(m[0, 1, rows, :], second[...], preferred_element_type=F32))
 
     def x_solve(f, first, second, n):
-        rows = at(n, CHUNK)
-        return (lax.dot_general(first, m[f, 0, rows, :], NT, preferred_element_type=F32)
-                + lax.dot_general(second, m[f, 1, rows, :], NT, preferred_element_type=F32))
+        columns = at(n, CHUNK)
+        return (jnp.dot(first, mt[f, 0, :, columns], preferred_element_type=F32)
+                + jnp.dot(second, mt[f, 1, :, columns], preferred_element_type=F32))
+
+    def flip_matrix(f):
+        def body(i, carry):
+            part = i // 8
+            r = lax.rem(i, 8)
+            mt[f, part, :, at(r, LANES)] = m[f, part, at(r, LANES), :].T
+            return carry
+
+        lax.fori_loop(0, 16, body, 0)
 
     def send_group(send, got, phase, n):
         def body(i, carry):
@@ -205,7 +232,8 @@
 
         lax.fori_loop(0, 8, body, 0)
 
-    loads[3].wait()
+    loads[5].wait()
+    flip_matrix(0)
     wait_on(rs.at[A2A1], got1.at[pl.ds(0, ROWS * (SHARDS - 1))])
     y_operands(got1, ya)
 
@@ -216,11 +244,13 @@
         return carry
 
     lax.fori_loop(0, 4, solve1, 0)
+    sent(A2A2, send2.at[pl.ds(0, BLOCK * (GROUP - 1))])
     got2[at(k, BLOCK), :] = send2[at(k, BLOCK), :]
 
     wait_on(rs.at[LENS1], lens1.at[0])
     forward1 = remote(lens1.at[core], lens1.at[core], FWD1, fq + 1 - 2 * core, s)
     forward1.start()
+    pending.append(forward1.wait_send)
 
     skew = jnp.where(mine, 0, 1)
 
@@ -234,6 +264,8 @@
         return carry
 
     lax.fori_loop(0, 32, go_lens2, 0)
+    sent(LENS2, lens2_send.at[pl.ds(0, ROWS * 31)], mine)
+    sent(LENS2, lens2_send, jnp.logical_not(mine))
 
     @pl.when(mine)
     def _():
@@ -289,6 +321,7 @@
         return carry
 
     lax.fori_loop(0, 4, solve3, 0)
+    sent(A2A3, send3.at[pl.ds(0, BLOCK * (GROUP - 1))])
     got3[at(k, BLOCK), :] = send3[at(k, BLOCK), :]
 
     def sum_send(part, total, phase):
@@ -300,6 +333,7 @@
             return carry
 
         lax.fori_loop(1, 8, body, 0)
+        sent(phase, part.at[pl.ds(0, 7)])
 
     def sum_up(total, phase):
         wait_on(rs.at[phase], total.at[pl.ds(0, 7)])
@@ -320,6 +354,8 @@
     @pl.when(jnp.logical_not(mine))
     def _():
         forward2.wait_recv()
+
+    sent(FWD2, lens2, mine)
 
     def trig2(i, carry):
         terms = lens2[at(i, 128), :].astype(F32)
@@ -333,11 +369,6 @@
         return carry
 
     lax.fori_loop(0, 8, trig2, 0)
-
-    dist0_send[...] = sum_up(sum0, SUM0).astype(BF16)
-    for f in range(4):
-        for b in range(2):
-            give(dist0_send.at[pl.ds(b * ROWS, ROWS)], dist0.at[rank], DIST0, f, 2 * k + b)
 
     wait_on(rs.at[A2A3], got3.at[pl.ds(0, BLOCK * (GROUP - 1))])
     y_operands(got3, ya)
@@ -378,7 +409,15 @@
         return carry
 
     lax.fori_loop(0, 4, solve5, 0)
+    sent(A2A4, send4.at[pl.ds(0, ROWS * (SHARDS - 1))])
     got4[at(s, ROWS), :] = send4[at(s, ROWS), :]
+
+    dist0_send[...] = sum_up(sum0, SUM0).astype(BF16)
+    for f in range(4):
+        for b in range(2):
+            give(dist0_send.at[pl.ds(b * ROWS, ROWS)], dist0.at[rank], DIST0, f, 2 * k + b)
+    sent(DIST0, dist0.at[pl.ds(0, 7)], own1)
+    sent(DIST0, dist0, jnp.logical_not(own1))
 
     total1 = sum_up(sum1, SUM1)
     for d in range(4):
@@ -393,8 +432,11 @@
         return carry
 
     lax.fori_loop(0, 32, go_dist1, 0)
-
-    loads[4].wait()
+    sent(DIST1, dist1.at[pl.ds(0, 31)], s // 8 == rank)
+    sent(DIST1, dist1, s // 8 != rank)
+
+    loads[6].wait()
+    flip_matrix(1)
     wait_on(rs.at[A2A4], got4.at[pl.ds(0, ROWS * (SHARDS - 1))])
 
     def gather4(i, carry):
@@ -408,23 +450,35 @@
 
     lax.fori_loop(0, 16, gather4, 0)
 
-    def solve6(n, carry):
+    def pair_copy(n):
+        return remote(pair.at[n, core], pair.at[n, core], PAIR + n, fq + 1 - 2 * core, s)
+
+    def cross_copy(n):
+        return remote(cross.at[n, z_hi], cross.at[n, z_hi], CROSS + n, lax.rem(fq + 2, 4), s)
+
+    def pass_on(n):
+        pair_copy(n).wait_recv()
+        cross[n, z_hi] = (pair[n, 0].astype(F32) + pair[n, 1].astype(F32)).astype(BF16)
+        cross_copy(n).start()
+        pending.append(pair_copy(n).wait_send)
+        pending.append(cross_copy(n).wait_send)
+
+    for n in range(4):
         image = jnp.zeros((ROWS, CHUNK), F32)
-        for f in range(2):
-            which = jnp.where(h == f, 0, 1)
-            new = x_solve(which, xf[f, 0], xf[f, 1], n)
+        for u in range(2):
+            f = h if u == 0 else 1 - h
+            new = x_solve(u, xf[f, 0], xf[f, 1], n)
             sre, sim, rre, rim = (new[c * ROWS:(c + 1) * ROWS] for c in range(4))
             src_out[0, f, :, at(n, CHUNK)] = sre.astype(BF16)
             src_out[1, f, :, at(n, CHUNK)] = sim.astype(BF16)
             rcv_out[0, f, :, at(n, CHUNK)] = rre.astype(BF16)
             rcv_out[1, f, :, at(n, CHUNK)] = rim.astype(BF16)
             image += wt[f] * (sre * rre + sim * rim)
-        pair[core, :, at(n, CHUNK)] = image.astype(BF16)
-        return carry
-
-    lax.fori_loop(0, 4, solve6, 0)
-    to_pair = remote(pair.at[core], pair.at[core], PAIR, fq + 1 - 2 * core, s)
-    to_pair.start()
+        pair[n, core] = image.astype(BF16)
+        pair_copy(n).start()
+        if n > 0:
+            pass_on(n - 1)
+    pass_on(3)
 
     wait_on(rs.at[DIST0], dist0)
     wait_on(rs.at[DIST1], dist1)
@@ -436,59 +490,12 @@
             tile = jnp.where(block == p, dist1[4 * j + p].astype(F32), tile)
         grad[1, :, pl.ds(j * LANES, LANES)] = tile
 
-    to_pair.wait_recv()
-    cross[z_hi] = (pair[0].astype(F32) + pair[1].astype(F32)).astype(BF16)
-    to_cross = remote(cross.at[z_hi], cross.at[z_hi], CROSS, lax.rem(fq + 2, 4), s)
-    to_cross.start()
-
-    wait_on(ss.at[A2A1], send1.at[pl.ds(0, ROWS * (SHARDS - 1))])
-    wait_on(ss.at[A2A2], send2.at[pl.ds(0, BLOCK * (GROUP - 1))])
-    wait_on(ss.at[A2A3], send3.at[pl.ds(0, BLOCK * (GROUP - 1))])
-    wait_on(ss.at[A2A4], send4.at[pl.ds(0, ROWS * (SHARDS - 1))])
-    wait_on(ss.at[SUM0], part0.at[pl.ds(0, 7)])
-    wait_on(ss.at[SUM1], part1.at[pl.ds(0, 7)])
-    forward1.wait_send()
-
-    own1 = (s == 0) | (s == SHARDS - 1)
-
-    @pl.when(mine & own1)
-    def _():
-        wait_on(ss.at[LENS1], lens_v.at[1])
-
-    @pl.when(mine & jnp.logical_not(own1))
-    def _():
-        wait_on(ss.at[LENS1], lens_v.at[pl.ds(0, 2)])
-
-    @pl.when(mine)
-    def _():
-        wait_on(ss.at[LENS2], lens2_send.at[pl.ds(0, ROWS * 31)])
-        forward2.wait_send()
-
-    @pl.when(jnp.logical_not(mine))
-    def _():
-        wait_on(ss.at[LENS2], lens2_send)
-
-    @pl.when(own1)
-    def _():
-        wait_on(ss.at[DIST0], dist0.at[pl.ds(0, 7)])
-
-    @pl.when(jnp.logical_not(own1))
-    def _():
-        wait_on(ss.at[DIST0], dist0)
-
-    own_dist = s // 8 == rank
-
-    @pl.when(own_dist)
-    def _():
-        wait_on(ss.at[DIST1], dist1.at[pl.ds(0, 31)])
-
-    @pl.when(jnp.logical_not(own_dist))
-    def _():
-        wait_on(ss.at[DIST1], dist1)
-
-    to_pair.wait_send()
-    to_cross.wait()
-    grad[2] = cross[0].astype(F32) + cross[1].astype(F32)
+    for wait in pending:
+        wait()
+
+    for n in range(4):
+        cross_copy(n).wait_recv()
+        grad[2, :, at(n, CHUNK)] = cross[n, 0].astype(F32) + cross[n, 1].astype(F32)
 
 
 def on_device(source_field, receiver_field, line_inverse, lens_delay, omegas, image_weights):
@@ -497,15 +504,15 @@
     return pl.pallas_call(
         kernel,
         out_shape=(
-            jax.ShapeDtypeStruct(source_field.shape, BF16),
-            jax.ShapeDtypeStruct(receiver_field.shape, BF16),
-            jax.ShapeDtypeStruct(lens_delay.shape, F32),
+            vmem(source_field.shape, BF16),
+            vmem(receiver_field.shape, BF16),
+            vmem(lens_delay.shape, F32),
         ),
-        in_specs=[pl.BlockSpec(memory_space=pl.ANY)] * 4 + [pl.BlockSpec(memory_space=pltpu.SMEM)] * 2,
+        in_specs=[pl.BlockSpec(memory_space=pl.ANY)] * 6,
         out_specs=[pl.BlockSpec(memory_space=vmem)] * 3,
         scratch_shapes=[
             vmem(source_field.shape, BF16), vmem(receiver_field.shape, BF16), vmem(lens_delay.shape, F32),
-            vmem((2, 2, NL, NL), BF16),
+            vmem((2, 2, NL, NL), BF16), vmem((2, 2, NL, NL), BF16),
             plane, plane, plane, plane, plane, plane, plane, plane,
             plane, vmem((2, NL, LANES), BF16),
             vmem((2, LANES, NL), BF16), vmem((2, LANES, NL), BF16), vmem((2, 2, 64, NL), BF16),
@@ -516,13 +523,14 @@
             vmem((BLOCK, LANES), BF16), vmem((8, ROWS, LANES), BF16),
             vmem((8, BLOCK, LANES), BF16), vmem((8, BLOCK, LANES), BF16),
             vmem((4, BLOCK, LANES), BF16), vmem((GROUP, ROWS, LANES), BF16),
-            vmem((2, ROWS, NL), BF16), vmem((2, ROWS, NL), BF16),
-            pltpu.SemaphoreType.DMA((5,)),
+            vmem((4, 2, ROWS, CHUNK), BF16), vmem((4, 2, ROWS, CHUNK), BF16),
+            pltpu.SMEM((2,), F32), pltpu.SMEM((2,), F32),
+            pltpu.SemaphoreType.DMA((7,)),
             pltpu.SemaphoreType.DMA((PHASES,)),
             pltpu.SemaphoreType.DMA((PHASES,)),
         ],
         compiler_params=pltpu.CompilerParams(
-            collective_id=0, has_side_effects=True, vmem_limit_bytes=40 * 2**20),
+            collective_id=0, has_side_effects=True, vmem_limit_bytes=60 * 2**20),
     )(source_field, receiver_field, line_inverse, lens_delay, omegas, image_weights)
 
 

time: 80.7 us -> 68.4 us (0.85)
  the two profiles are of different devices: /device:TPU:33 before, /device:TPU:38 now
where the time goes in v2:
time: 68.4 us; the launch traced here: 68.3 us
  Pallas kernels  65.7 us (96%)
  local copies, waits for them, and re-layouts  1.99 us (3%)
    pallas_call x1, Pallas kernels, on_device(): pl.pallas_call(kernel, out_shape=(vmem(source_field.shape, BF16), vmem(re...  65.7 us
    unnamed x3, local copies, waits for them, and re-layouts  1.99 us

profile of v2, /device:TPU:38, one launch (start us, length us, event | category | flops | bytes accessed | tf_op | source)
XLA Modules:
  0.0 68.3 jit_solution(4216517340846958633)
XLA Ops:
  0.6 65.7 %shard_map.85 = (bf16[2,2,16,1024]{3,2,1,0:T(8,128)(2,1)S(1)}, bf16[2,2,16,1024]{3,2,1,0:T(8,128)(2,1)S(1)}, f32[3,16,1024]{2,1,0:T(8,128)S(1)}) custom-call(bf16[2,2,16,1024]{3,2,1,0:T(8,128)(2,1)} %src.1, bf16[2,2,16,1024]{3,2,1,0:T(8,128)(2,1)} %rcv.1, bf16[2,2,1024,1024]{3,2,1,0:T(8,128)(2,1)} %minv.1, f32[3,16,1024]{2,1,0:T(8,128)} %lens.1, f32[2]{0:T(128)} %om_hbm.1, ...), custom_call_target="tpu_custom_call" | custom-call | tf_op jit(solution)/shard_map/pallas_call | solution.py:504
  66.3 0.7 copy.12
  67.0 0.7 copy.13
  67.6 0.7 copy.14

commit v3 on v2

--- a/solution.py
+++ b/solution.py
@@ -75,11 +75,12 @@
     return pl.ds(start if isinstance(start, int) else pl.multiple_of(start, size), size)
 
 
-def kernel(src, rcv, minv, lens, om_hbm, wt_hbm, src_out, rcv_out, grad,
+def kernel(src, rcv, minv, lens, om_hbm, wt_hbm, fields, grad,
            src_v, rcv_v, lens_v, m, mt, send1, got1, send2, got2, send3, got3, send4, got4,
-           ya, yb, xa, xb, xf, cos1, sin1, cos2, sin2, lens1, lens2_send, lens2,
+           ya, yb, xa, xb, xf, acc_y, acc_x, acc_f, cos1, sin1, cos2, sin2, lens1, lens2_send, lens2,
            part0, sum0, dist0_send, dist0, part1, sum1, dist1_send, dist1,
-           pair, cross, om, wt, load_sem, ss, rs):
+           pair, cross, om, wt, load_sem, ss, rs, parts):
+    src_out, rcv_out = fields.at[0], fields.at[1]
     fq = lax.axis_index("freq")
     s = lax.axis_index("space")
     h = s // GROUP
@@ -93,6 +94,14 @@
         return pltpu.make_async_remote_copy(
             src_ref=source, dst_ref=target, send_sem=ss.at[phase], recv_sem=rs.at[phase],
             device_id={"freq": freq, "space": space}, device_id_type=MESH)
+
+    quarter = k // 8
+    plane = s // 16
+
+    def transposed(source, target, phase, part, space):
+        pltpu.make_async_remote_copy(
+            src_ref=source, dst_ref=target, send_sem=ss.at[phase], recv_sem=parts.at[4 * phase + part],
+            device_id={"freq": fq, "space": space}, device_id_type=MESH).start()
 
     def wait_on(sem, ref):
         pltpu.make_async_copy(ref, ref, sem).wait()
@@ -165,12 +174,23 @@
     got1[at(s, ROWS), :] = send1[at(s, ROWS), :]
     pl.semaphore_wait(barrier, SHARDS - 1 + 3)
 
+    def send_all(send, got, phase, n):
+        def body(i, carry):
+            t = n * 16 + lax.rem(s + i, 16)
+
+            @pl.when(t != s)
+            def _():
+                transposed(send.at[at(t, ROWS)], got.at[at(s, ROWS)], phase, plane, t)
+
+            return carry
+
+        lax.fori_loop(0, 16, body, 0)
+
     def go1(i, carry):
-        t = lax.rem(s + i, SHARDS)
-        remote(send1.at[at(t, ROWS)], got1.at[at(s, ROWS)], A2A1, fq, t).start()
-        return carry
-
-    lax.fori_loop(1, SHARDS, go1, 0)
+        send_all(send1, got1, A2A1, lax.rem(plane + i, 4))
+        return carry
+
+    lax.fori_loop(0, 4, go1, 0)
     sent(A2A1, send1.at[pl.ds(0, ROWS * (SHARDS - 1))])
 
     @pl.when(mine)
@@ -193,13 +213,48 @@
 
     lax.fori_loop(0, 8, pack2, 0)
 
-    def y_operands(got, other):
-        def body(i, carry):
-            tile = got[at(i, 128), :].astype(F32)
-            other[at(i, 128), :] = (swap_parts(tile) * outer_sign(tile)).astype(BF16)
-            return carry
-
-        lax.fori_loop(0, 8, body, 0)
+    def arrivals(phase, got, own, lines, use, last):
+        for i in range(4):
+            g = lax.rem(own + 4 - i, 4)
+            wait_on(parts.at[4 * phase + g], got.at[pl.ds(0, CHUNK - (lines if i == 0 else 0))])
+            if i < 3:
+                use(g, i)
+            else:
+                last(g)
+
+    def y_operands(got, other, g):
+        for u in range(2):
+            rows = at(2 * g + u, 128)
+            tile = got[rows, :].astype(F32)
+            other[rows, :] = (swap_parts(tile) * outer_sign(tile)).astype(BF16)
+
+    def y_arrivals(phase, got, own, lines, start, finish):
+        def part(g, rows):
+            return (jnp.dot(m[0, 0, rows, at(g, CHUNK)], got[at(g, CHUNK), :], preferred_element_type=F32)
+                    + jnp.dot(m[0, 1, rows, at(g, CHUNK)], ya[at(g, CHUNK), :], preferred_element_type=F32))
+
+        def use(g, i):
+            y_operands(got, ya, g)
+
+            def body(n, carry):
+                rows = at(n, CHUNK)
+                acc_y[rows, :] = part(g, rows) if i == 0 else acc_y[rows, :] + part(g, rows)
+                return carry
+
+            lax.fori_loop(0, 4, body, 0)
+
+        def last(g):
+            y_operands(got, ya, g)
+
+            def body(i, carry):
+                n = lax.rem(start + i, 4)
+                rows = at(n, CHUNK)
+                finish(n, acc_y[rows, :] + part(g, rows))
+                return carry
+
+            lax.fori_loop(0, 4, body, 0)
+
+        arrivals(phase, got, own, lines, use, last)
 
     def y_solve(first, second, n):
         rows = at(n, CHUNK)
@@ -211,14 +266,14 @@
         return (jnp.dot(first, mt[f, 0, :, columns], preferred_element_type=F32)
                 + jnp.dot(second, mt[f, 1, :, columns], preferred_element_type=F32))
 
-    def flip_matrix(f):
+    def flip_matrix(f, begin, end):
         def body(i, carry):
             part = i // 8
             r = lax.rem(i, 8)
             mt[f, part, :, at(r, LANES)] = m[f, part, at(r, LANES), :].T
             return carry
 
-        lax.fori_loop(0, 16, body, 0)
+        lax.fori_loop(begin, end, body, 0)
 
     def send_group(send, got, phase, n):
         def body(i, carry):
@@ -226,24 +281,20 @@
 
             @pl.when(t != k)
             def _():
-                remote(send.at[at(t, BLOCK)], got.at[at(k, BLOCK)], phase, fq, h * GROUP + t).start()
+                transposed(send.at[at(t, BLOCK)], got.at[at(k, BLOCK)], phase, quarter, h * GROUP + t)
 
             return carry
 
         lax.fori_loop(0, 8, body, 0)
 
     loads[5].wait()
-    flip_matrix(0)
-    wait_on(rs.at[A2A1], got1.at[pl.ds(0, ROWS * (SHARDS - 1))])
-    y_operands(got1, ya)
-
-    def solve1(i, carry):
-        n = lax.rem(k // 8 + i, 4)
-        send2[at(n, CHUNK), :] = y_solve(got1, ya, n).astype(BF16)
+    flip_matrix(0, 0, 16)
+
+    def finish1(n, new):
+        send2[at(n, CHUNK), :] = new.astype(BF16)
         send_group(send2, got2, A2A2, n)
-        return carry
-
-    lax.fori_loop(0, 4, solve1, 0)
+
+    y_arrivals(A2A1, got1, plane, ROWS, quarter, finish1)
     sent(A2A2, send2.at[pl.ds(0, BLOCK * (GROUP - 1))])
     got2[at(k, BLOCK), :] = send2[at(k, BLOCK), :]
 
@@ -281,20 +332,42 @@
         return carry
 
     lax.fori_loop(0, 8, trig1, 0)
-
-    wait_on(rs.at[A2A2], got2.at[pl.ds(0, BLOCK * (GROUP - 1))])
-
-    def gather2(q, carry):
-        tiles = block_transpose([got2[at(4 * q + p, BLOCK), :].astype(F32) for p in range(4)])
-        for c in range(4):
-            xa[0, pl.ds(c * BLOCK, BLOCK), at(q, LANES)] = tiles[c].astype(BF16)
-            xa[1, pl.ds(c * BLOCK, BLOCK), at(q, LANES)] = (SWAP_SIGN[c] * tiles[c ^ 1]).astype(BF16)
-        return carry
-
-    lax.fori_loop(0, 8, gather2, 0)
-
-    def solve2(n, carry):
-        new = x_solve(0, xa[0], xa[1], n)
+    loads[6].wait()
+    flip_matrix(1, 0, 8)
+
+    def gather2(g):
+        for u in range(2):
+            q = 2 * g + u
+            tiles = block_transpose([got2[at(4 * q + p, BLOCK), :].astype(F32) for p in range(4)])
+            for c in range(4):
+                xa[0, pl.ds(c * BLOCK, BLOCK), at(q, LANES)] = tiles[c].astype(BF16)
+                xa[1, pl.ds(c * BLOCK, BLOCK), at(q, LANES)] = (SWAP_SIGN[c] * tiles[c ^ 1]).astype(BF16)
+
+    def x_part(g, columns):
+        return (jnp.dot(xa[0, :, at(g, CHUNK)], mt[0, 0, at(g, CHUNK), columns], preferred_element_type=F32)
+                + jnp.dot(xa[1, :, at(g, CHUNK)], mt[0, 1, at(g, CHUNK), columns],
+                          preferred_element_type=F32))
+
+    def use2(g, i):
+        gather2(g)
+
+        def body(n, carry):
+            columns = at(n, CHUNK)
+            acc_x[:, columns] = x_part(g, columns) if i == 0 else acc_x[:, columns] + x_part(g, columns)
+            return carry
+
+        lax.fori_loop(0, 4, body, 0)
+
+    def last2(g):
+        gather2(g)
+
+        def body(n, carry):
+            solve2(n, acc_x[:, at(n, CHUNK)] + x_part(g, at(n, CHUNK)))
+            return carry
+
+        lax.fori_loop(0, 4, body, 0)
+
+    def solve2(n, new):
         sre, sim, rre, rim = (new[c * BLOCK:(c + 1) * BLOCK] for c in range(4))
         image = wt_h * (sre * rre + sim * rim)
         for u in range(2):
@@ -305,9 +378,8 @@
             xb[0, pl.ds(part * BLOCK, BLOCK), at(n, CHUNK)] = turned[part].astype(BF16)
             xb[1, pl.ds(part * BLOCK, BLOCK), at(n, CHUNK)] = (
                 SWAP_SIGN[part] * turned[part ^ 1]).astype(BF16)
-        return carry
-
-    lax.fori_loop(0, 4, solve2, 0)
+
+    arrivals(A2A2, got2, quarter, BLOCK, use2, last2)
 
     def solve3(i, carry):
         n = lax.rem(k // 8 + i, 4)
@@ -369,12 +441,9 @@
         return carry
 
     lax.fori_loop(0, 8, trig2, 0)
-
-    wait_on(rs.at[A2A3], got3.at[pl.ds(0, BLOCK * (GROUP - 1))])
-    y_operands(got3, ya)
-
-    def solve4(n, carry):
-        new = y_solve(got3, ya, n)
+    flip_matrix(1, 8, 16)
+
+    def solve4(n, new):
         product = wt_h * new * turn(new, 64)
         image = product + turn(product, -32)
         for u in range(2):
@@ -387,25 +456,15 @@
         turned = new * cos2[at(n, CHUNK), :] + swap_parts(new) * sin2[at(n, CHUNK), :]
         yb[0, at(n, CHUNK), :] = turned.astype(BF16)
         yb[1, at(n, CHUNK), :] = (swap_parts(turned) * outer_sign(turned)).astype(BF16)
-        return carry
-
-    lax.fori_loop(0, 4, solve4, 0)
+
+    y_arrivals(A2A3, got3, quarter, BLOCK, 0, solve4)
     sum_send(part1, sum1, SUM1)
 
     def solve5(i, carry):
-        n = lax.rem(s // 16 + i, 4)
+        n = lax.rem(plane + i, 4)
         send4[at(n, CHUNK), :] = y_solve(yb.at[0], yb.at[1], n).astype(BF16)
 
-        def body(j, inner):
-            t = n * 16 + lax.rem(s + j, 16)
-
-            @pl.when(t != s)
-            def _():
-                remote(send4.at[at(t, ROWS)], got4.at[at(s, ROWS)], A2A4, fq, t).start()
-
-            return inner
-
-        lax.fori_loop(0, 16, body, 0)
+        send_all(send4, got4, A2A4, n)
         return carry
 
     lax.fori_loop(0, 4, solve5, 0)
@@ -435,20 +494,32 @@
     sent(DIST1, dist1.at[pl.ds(0, 31)], s // 8 == rank)
     sent(DIST1, dist1, s // 8 != rank)
 
-    loads[6].wait()
-    flip_matrix(1)
-    wait_on(rs.at[A2A4], got4.at[pl.ds(0, ROWS * (SHARDS - 1))])
-
-    def gather4(i, carry):
-        f = i // 8
-        q = lax.rem(i, 8)
-        tiles = block_transpose([got4[at(f * GROUP + 4 * q + p, ROWS), :].astype(F32) for p in range(4)])
-        for c in range(4):
-            xf[f, 0, pl.ds(c * ROWS, ROWS), at(q, LANES)] = tiles[c].astype(BF16)
-            xf[f, 1, pl.ds(c * ROWS, ROWS), at(q, LANES)] = (SWAP_SIGN[c] * tiles[c ^ 1]).astype(BF16)
-        return carry
-
-    lax.fori_loop(0, 16, gather4, 0)
+    acc_f[...] = jnp.zeros_like(acc_f)
+
+    def gather4(g):
+        f = g // 2
+        for u in range(4):
+            q = 4 * lax.rem(g, 2) + u
+            tiles = block_transpose([got4[at(f * GROUP + 4 * q + p, ROWS), :].astype(F32) for p in range(4)])
+            for c in range(4):
+                xf[f, 0, pl.ds(c * ROWS, ROWS), at(q, LANES)] = tiles[c].astype(BF16)
+                xf[f, 1, pl.ds(c * ROWS, ROWS), at(q, LANES)] = (SWAP_SIGN[c] * tiles[c ^ 1]).astype(BF16)
+
+    def f_part(g, columns):
+        f = g // 2
+        which = jnp.where(h == f, 0, 1)
+        terms = at(lax.rem(g, 2), 512)
+        return (jnp.dot(xf[f, 0, :, terms], mt[which, 0, terms, columns], preferred_element_type=F32)
+                + jnp.dot(xf[f, 1, :, terms], mt[which, 1, terms, columns], preferred_element_type=F32))
+
+    def use4(g, i):
+        gather4(g)
+
+        def body(n, carry):
+            acc_f[g // 2, :, at(n, CHUNK)] += f_part(g, at(n, CHUNK))
+            return carry
+
+        lax.fori_loop(0, 4, body, 0)
 
     def pair_copy(n):
         return remote(pair.at[n, core], pair.at[n, core], PAIR + n, fq + 1 - 2 * core, s)
@@ -463,22 +534,28 @@
         pending.append(pair_copy(n).wait_send)
         pending.append(cross_copy(n).wait_send)
 
-    for n in range(4):
-        image = jnp.zeros((ROWS, CHUNK), F32)
-        for u in range(2):
-            f = h if u == 0 else 1 - h
-            new = x_solve(u, xf[f, 0], xf[f, 1], n)
-            sre, sim, rre, rim = (new[c * ROWS:(c + 1) * ROWS] for c in range(4))
-            src_out[0, f, :, at(n, CHUNK)] = sre.astype(BF16)
-            src_out[1, f, :, at(n, CHUNK)] = sim.astype(BF16)
-            rcv_out[0, f, :, at(n, CHUNK)] = rre.astype(BF16)
-            rcv_out[1, f, :, at(n, CHUNK)] = rim.astype(BF16)
-            image += wt[f] * (sre * rre + sim * rim)
-        pair[n, core] = image.astype(BF16)
-        pair_copy(n).start()
-        if n > 0:
-            pass_on(n - 1)
-    pass_on(3)
+    def last4(g):
+        gather4(g)
+        for n in range(4):
+            image = jnp.zeros((ROWS, CHUNK), F32)
+            for u in range(2):
+                f = g // 2 if u == 0 else 1 - g // 2
+                new = acc_f[f, :, at(n, CHUNK)]
+                if u == 0:
+                    new += f_part(g, at(n, CHUNK))
+                sre, sim, rre, rim = (new[c * ROWS:(c + 1) * ROWS] for c in range(4))
+                src_out[0, f, :, at(n, CHUNK)] = sre.astype(BF16)
+                src_out[1, f, :, at(n, CHUNK)] = sim.astype(BF16)
+                rcv_out[0, f, :, at(n, CHUNK)] = rre.astype(BF16)
+                rcv_out[1, f, :, at(n, CHUNK)] = rim.astype(BF16)
+                image += wt[f] * (sre * rre + sim * rim)
+            pair[n, core] = image.astype(BF16)
+            pair_copy(n).start()
+            if n > 0:
+                pass_on(n - 1)
+        pass_on(3)
+
+    arrivals(A2A4, got4, plane, ROWS, use4, last4)
 
     wait_on(rs.at[DIST0], dist0)
     wait_on(rs.at[DIST1], dist1)
@@ -501,21 +578,21 @@
 def on_device(source_field, receiver_field, line_inverse, lens_delay, omegas, image_weights):
     vmem = pltpu.VMEM
     plane = vmem((NL, LANES), BF16)
-    return pl.pallas_call(
+    fields, gradient = pl.pallas_call(
         kernel,
         out_shape=(
-            vmem(source_field.shape, BF16),
-            vmem(receiver_field.shape, BF16),
+            vmem((2,) + source_field.shape, BF16),
             vmem(lens_delay.shape, F32),
         ),
         in_specs=[pl.BlockSpec(memory_space=pl.ANY)] * 6,
-        out_specs=[pl.BlockSpec(memory_space=vmem)] * 3,
+        out_specs=[pl.BlockSpec(memory_space=vmem)] * 2,
         scratch_shapes=[
             vmem(source_field.shape, BF16), vmem(receiver_field.shape, BF16), vmem(lens_delay.shape, F32),
             vmem((2, 2, NL, NL), BF16), vmem((2, 2, NL, NL), BF16),
             plane, plane, plane, plane, plane, plane, plane, plane,
             plane, vmem((2, NL, LANES), BF16),
             vmem((2, LANES, NL), BF16), vmem((2, LANES, NL), BF16), vmem((2, 2, 64, NL), BF16),
+            vmem((NL, LANES), F32), vmem((LANES, NL), F32), vmem((2, 64, NL), F32),
             vmem((BLOCK, NL), F32), vmem((BLOCK, NL), F32),
             vmem((NL, LANES), F32), vmem((NL, LANES), F32),
             vmem((2, ROWS, NL), F32), vmem((GROUP * ROWS, LANES), BF16), plane,
@@ -528,10 +605,12 @@
             pltpu.SemaphoreType.DMA((7,)),
             pltpu.SemaphoreType.DMA((PHASES,)),
             pltpu.SemaphoreType.DMA((PHASES,)),
+            pltpu.SemaphoreType.DMA((16,)),
         ],
         compiler_params=pltpu.CompilerParams(
             collective_id=0, has_side_effects=True, vmem_limit_bytes=60 * 2**20),
     )(source_field, receiver_field, line_inverse, lens_delay, omegas, image_weights)
+    return fields[0], fields[1], gradient
 
 
 def solution(mesh):

time: 68.4 us -> 66.5 us (0.972)
  the two profiles are of different devices: /device:TPU:38 before, /device:TPU:1 now
where the time goes in v3:
time: 66.5 us
  Pallas kernels  64.4 us (97%)
  local copies, waits for them, and re-layouts  1.39 us (2%)
    pallas_call x1, Pallas kernels, on_device(): pl.pallas_call(kernel, out_shape=(vmem((2,) + source_field.shape, BF16),...  64.4 us

profile of v3, /device:TPU:1, one launch (start us, length us, event | category | flops | bytes accessed | tf_op | source)
XLA Modules:
  0.0 66.5 jit_solution(3302461167114905182)
XLA Ops:
  0.6 64.4 %shard_map.85 = (bf16[2,2,2,16,1024]{4,3,2,1,0:T(8,128)(2,1)S(1)}, f32[3,16,1024]{2,1,0:T(8,128)S(1)}) custom-call(bf16[2,2,16,1024]{3,2,1,0:T(8,128)(2,1)} %src.1, bf16[2,2,16,1024]{3,2,1,0:T(8,128)(2,1)} %rcv.1, bf16[2,2,1024,1024]{3,2,1,0:T(8,128)(2,1)} %minv.1, f32[3,16,1024]{2,1,0:T(8,128)} %lens.1, f32[2]{0:T(128)} %om_hbm.1, f32[2]{0:T(128)} %wt_hbm.1), custom_call_target="tpu_custom_call" | custom-call | tf_op jit(solution)/shard_map/pallas_call | solution.py:581
  65.1 0.7 %slice_bitcast_fusion = (bf16[2,2,16,1024]{3,2,1,0:T(8,128)(2,1)}, bf16[2,2,16,1024]{3,2,1,0:T(8,128)(2,1)}) fusion(bf16[2,2,2,16,1024]{4,3,2,1,0:T(8,128)(2,1)S(1)} %get-tuple-element.5), kind=kLoop, calls=%fused_computation | loop fusion | bytes 524288 | tf_op jit(solution)/shard_map/squeeze | solution.py:613
  65.8 0.7 %copy.10 = f32[3,16,1024]{2,1,0:T(8,128)} copy(f32[3,16,1024]{2,1,0:T(8,128)S(1)} %get-tuple-element.11) | data formatting | bytes 393216

commit v4 on v3

--- a/solution.py
+++ b/solution.py
@@ -18,8 +18,8 @@
 SWAP_SIGN = (-1.0, 1.0, 1.0, -1.0)
 
 (A2A1, A2A2, A2A3, A2A4, LENS1, LENS2, FWD1, FWD2,
- SUM0, DIST0, SUM1, DIST1, PAIR, _, _, _, CROSS, _, _, _) = range(20)
-PHASES = 20
+ SUM0, DIST0, SUM1, DIST1, PAIR, _, _, _, CROSS, _, _, _, HAND0, HAND1) = range(22)
+PHASES = 22
 
 
 def lanes(tile):
@@ -175,16 +175,13 @@
     pl.semaphore_wait(barrier, SHARDS - 1 + 3)
 
     def send_all(send, got, phase, n):
-        def body(i, carry):
+        def one(i):
             t = n * 16 + lax.rem(s + i, 16)
-
-            @pl.when(t != s)
-            def _():
-                transposed(send.at[at(t, ROWS)], got.at[at(s, ROWS)], phase, plane, t)
-
-            return carry
-
-        lax.fori_loop(0, 16, body, 0)
+            transposed(send.at[at(t, ROWS)], got.at[at(s, ROWS)], phase, plane, t)
+
+        pl.when(n != plane)(lambda: one(0))
+        for i in range(1, 16):
+            one(i)
 
     def go1(i, carry):
         send_all(send1, got1, A2A1, lax.rem(plane + i, 4))
@@ -276,16 +273,13 @@
         lax.fori_loop(begin, end, body, 0)
 
     def send_group(send, got, phase, n):
-        def body(i, carry):
+        def one(i):
             t = n * 8 + lax.rem(k + i, 8)
-
-            @pl.when(t != k)
-            def _():
-                transposed(send.at[at(t, BLOCK)], got.at[at(k, BLOCK)], phase, quarter, h * GROUP + t)
-
-            return carry
-
-        lax.fori_loop(0, 8, body, 0)
+            transposed(send.at[at(t, BLOCK)], got.at[at(k, BLOCK)], phase, quarter, h * GROUP + t)
+
+        pl.when(n != quarter)(lambda: one(0))
+        for i in range(1, 8):
+            one(i)
 
     loads[5].wait()
     flip_matrix(0, 0, 16)
@@ -305,16 +299,13 @@
 
     skew = jnp.where(mine, 0, 1)
 
-    def go_lens2(i, carry):
+    def go_lens2(i):
         t = lax.rem(s + skew + 2 * i, SHARDS)
-
-        @pl.when(t != s)
-        def _():
-            remote(lens2_send.at[at(lax.rem(t, GROUP), ROWS)], lens2.at[at(s, ROWS)], LENS2, fq, t).start()
-
-        return carry
-
-    lax.fori_loop(0, 32, go_lens2, 0)
+        remote(lens2_send.at[at(lax.rem(t, GROUP), ROWS)], lens2.at[at(s, ROWS)], LENS2, fq, t).start()
+
+    pl.when(jnp.logical_not(mine))(lambda: go_lens2(0))
+    for i in range(1, 32):
+        go_lens2(i)
     sent(LENS2, lens2_send.at[pl.ds(0, ROWS * 31)], mine)
     sent(LENS2, lens2_send, jnp.logical_not(mine))
 
@@ -472,27 +463,29 @@
     got4[at(s, ROWS), :] = send4[at(s, ROWS), :]
 
     dist0_send[...] = sum_up(sum0, SUM0).astype(BF16)
-    for f in range(4):
+    for up in range(2):
         for b in range(2):
-            give(dist0_send.at[pl.ds(b * ROWS, ROWS)], dist0.at[rank], DIST0, f, 2 * k + b)
-    sent(DIST0, dist0.at[pl.ds(0, 7)], own1)
-    sent(DIST0, dist0, jnp.logical_not(own1))
+            give(dist0_send.at[pl.ds(b * ROWS, ROWS)], dist0.at[h, fq], DIST0, 2 * up + h, 2 * k + b)
+    sent(DIST0, dist0.at[0, pl.ds(0, 3)], own1 & (core == h))
+    sent(DIST0, dist0.at[0], jnp.logical_not(own1 & (core == h)))
 
     total1 = sum_up(sum1, SUM1)
     for d in range(4):
         dist1_send[d] = turn(total1, d * BLOCK).astype(BF16)
 
-    def go_dist1(i, carry):
-        f = i // 8
-        a = lax.rem(i, 8) // 2
-        b = lax.rem(i, 2)
-        d = lax.rem(k + 4 - a, 4)
-        give(dist1_send.at[d, at(b, ROWS)], dist1.at[k], DIST1, f, 8 * rank + lax.rem(i, 8))
-        return carry
-
-    lax.fori_loop(0, 32, go_dist1, 0)
-    sent(DIST1, dist1.at[pl.ds(0, 31)], s // 8 == rank)
-    sent(DIST1, dist1, s // 8 != rank)
+    side = lax.rem(k, 2)
+
+    def dist1_copy(i):
+        d = lax.rem(k + 4 - i // 2, 4)
+        return dist1_send.at[d, at(i % 2, ROWS)], dist1.at[side, k // 2], DIST1
+
+    for i in range(8):
+        remote(*dist1_copy(i), side + 2 * (1 - z_hi), 8 * rank + i).start()
+    for i in range(8):
+        give(*dist1_copy(i), side + 2 * z_hi, 8 * rank + i)
+    own_dist = (s // 8 == rank) & (core == side)
+    sent(DIST1, dist1.at[0, pl.ds(0, 15)], own_dist)
+    sent(DIST1, dist1.at[0], jnp.logical_not(own_dist))
 
     acc_f[...] = jnp.zeros_like(acc_f)
 
@@ -557,14 +550,21 @@
 
     arrivals(A2A4, got4, plane, ROWS, use4, last4)
 
-    wait_on(rs.at[DIST0], dist0)
-    wait_on(rs.at[DIST1], dist1)
+    wait_on(rs.at[DIST0], dist0.at[0])
+    wait_on(rs.at[DIST1], dist1.at[0])
+    hands = [remote(dist0.at[core], dist0.at[core], HAND0, fq + 1 - 2 * core, s),
+             remote(dist1.at[core], dist1.at[core], HAND1, fq + 1 - 2 * core, s)]
+    for hand in hands:
+        hand.start()
+        pending.append(hand.wait_send)
+    for hand in hands:
+        hand.wait_recv()
     for j in range(8):
-        grad[0, :, pl.ds(j * LANES, LANES)] = dist0[j].astype(F32)
-        tile = dist1[4 * j].astype(F32)
+        grad[0, :, pl.ds(j * LANES, LANES)] = dist0[j % 2, j // 2].astype(F32)
+        tile = dist1[0, 2 * j].astype(F32)
         block = lanes(tile) // BLOCK
         for p in range(1, 4):
-            tile = jnp.where(block == p, dist1[4 * j + p].astype(F32), tile)
+            tile = jnp.where(block == p, dist1[p % 2, 2 * j + p // 2].astype(F32), tile)
         grad[1, :, pl.ds(j * LANES, LANES)] = tile
 
     for wait in pending:
@@ -597,9 +597,9 @@
             vmem((NL, LANES), F32), vmem((NL, LANES), F32),
             vmem((2, ROWS, NL), F32), vmem((GROUP * ROWS, LANES), BF16), plane,
             vmem((8, BLOCK, LANES), BF16), vmem((8, BLOCK, LANES), BF16),
-            vmem((BLOCK, LANES), BF16), vmem((8, ROWS, LANES), BF16),
+            vmem((BLOCK, LANES), BF16), vmem((2, 4, ROWS, LANES), BF16),
             vmem((8, BLOCK, LANES), BF16), vmem((8, BLOCK, LANES), BF16),
-            vmem((4, BLOCK, LANES), BF16), vmem((GROUP, ROWS, LANES), BF16),
+            vmem((4, BLOCK, LANES), BF16), vmem((2, GROUP // 2, ROWS, LANES), BF16),
             vmem((4, 2, ROWS, CHUNK), BF16), vmem((4, 2, ROWS, CHUNK), BF16),
             pltpu.SMEM((2,), F32), pltpu.SMEM((2,), F32),
             pltpu.SemaphoreType.DMA((7,)),

time: 66.5 us -> 65.9 us (level)
  no operation moved by 1% of the time
where the time goes in v4:
time: 65.9 us; the launch traced here: 65.8 us
  Pallas kernels  63.8 us (97%)
  local copies, waits for them, and re-layouts  1.39 us (2%)
    pallas_call x1, Pallas kernels, on_device(): pl.pallas_call(kernel, out_shape=(vmem((2,) + source_field.shape, BF16),...  63.8 us

profile of v4, /device:TPU:1, one launch (start us, length us, event | category | flops | bytes accessed | tf_op | source)
XLA Modules:
  0.0 65.8 jit_solution(2823412317306121983)
XLA Ops:
  0.6 63.8 %shard_map.85 = (bf16[2,2,2,16,1024]{4,3,2,1,0:T(8,128)(2,1)S(1)}, f32[3,16,1024]{2,1,0:T(8,128)S(1)}) custom-call(bf16[2,2,16,1024]{3,2,1,0:T(8,128)(2,1)} %src.1, bf16[2,2,16,1024]{3,2,1,0:T(8,128)(2,1)} %rcv.1, bf16[2,2,1024,1024]{3,2,1,0:T(8,128)(2,1)} %minv.1, f32[3,16,1024]{2,1,0:T(8,128)} %lens.1, f32[2]{0:T(128)} %om_hbm.1, f32[2]{0:T(128)} %wt_hbm.1), custom_call_target="tpu_custom_call" | custom-call | tf_op jit(solution)/shard_map/pallas_call | solution.py:581
  64.4 0.7 %slice_bitcast_fusion = (bf16[2,2,16,1024]{3,2,1,0:T(8,128)(2,1)}, bf16[2,2,16,1024]{3,2,1,0:T(8,128)(2,1)}) fusion(bf16[2,2,2,16,1024]{4,3,2,1,0:T(8,128)(2,1)S(1)} %get-tuple-element.5), kind=kLoop, calls=%fused_computation | loop fusion | bytes 524288 | tf_op jit(solution)/shard_map/squeeze | solution.py:613
  65.1 0.7 %copy.10 = f32[3,16,1024]{2,1,0:T(8,128)} copy(f32[3,16,1024]{2,1,0:T(8,128)S(1)} %get-tuple-element.11) | data formatting | bytes 393216

commit v5 on v4

--- a/solution.py
+++ b/solution.py
@@ -283,6 +283,8 @@
 
     loads[5].wait()
     flip_matrix(0, 0, 16)
+    loads[6].wait()
+    flip_matrix(1, 0, 16)
 
     def finish1(n, new):
         send2[at(n, CHUNK), :] = new.astype(BF16)
@@ -323,8 +325,6 @@
         return carry
 
     lax.fori_loop(0, 8, trig1, 0)
-    loads[6].wait()
-    flip_matrix(1, 0, 8)
 
     def gather2(g):
         for u in range(2):
@@ -432,7 +432,6 @@
         return carry
 
     lax.fori_loop(0, 8, trig2, 0)
-    flip_matrix(1, 8, 16)
 
     def solve4(n, new):
         product = wt_h * new * turn(new, 64)
@@ -544,9 +543,8 @@
                 image += wt[f] * (sre * rre + sim * rim)
             pair[n, core] = image.astype(BF16)
             pair_copy(n).start()
-            if n > 0:
-                pass_on(n - 1)
-        pass_on(3)
+        for n in range(4):
+            pass_on(n)
 
     arrivals(A2A4, got4, plane, ROWS, use4, last4)
 

time: 65.9 us -> 64.6 us (0.980)
  Pallas kernels: 63.8 us -> 62.5 us
    pallas_call x1, Pallas kernels: 63.8 us -> 62.5 us  [on_device(): pl.pallas_call(kernel, out_shape=(vmem((2,) + source_field.shape, BF16),...]
where the time goes in v5:
time: 64.6 us
  Pallas kernels  62.5 us (97%)
  local copies, waits for them, and re-layouts  1.39 us (2%)
    pallas_call x1, Pallas kernels, on_device(): pl.pallas_call(kernel, out_shape=(vmem((2,) + source_field.shape, BF16),...  62.5 us

profile of v5, /device:TPU:1, one launch (start us, length us, event | category | flops | bytes accessed | tf_op | source)
XLA Modules:
  0.0 64.6 jit_solution(12522930054268290844)
XLA Ops:
  0.6 62.5 %shard_map.85 = (bf16[2,2,2,16,1024]{4,3,2,1,0:T(8,128)(2,1)S(1)}, f32[3,16,1024]{2,1,0:T(8,128)S(1)}) custom-call(bf16[2,2,16,1024]{3,2,1,0:T(8,128)(2,1)} %src.1, bf16[2,2,16,1024]{3,2,1,0:T(8,128)(2,1)} %rcv.1, bf16[2,2,1024,1024]{3,2,1,0:T(8,128)(2,1)} %minv.1, f32[3,16,1024]{2,1,0:T(8,128)} %lens.1, f32[2]{0:T(128)} %om_hbm.1, f32[2]{0:T(128)} %wt_hbm.1), custom_call_target="tpu_custom_call" | custom-call | tf_op jit(solution)/shard_map/pallas_call | solution.py:579
  63.2 0.7 %slice_bitcast_fusion = (bf16[2,2,16,1024]{3,2,1,0:T(8,128)(2,1)}, bf16[2,2,16,1024]{3,2,1,0:T(8,128)(2,1)}) fusion(bf16[2,2,2,16,1024]{4,3,2,1,0:T(8,128)(2,1)S(1)} %get-tuple-element.5), kind=kLoop, calls=%fused_computation | loop fusion | bytes 524288 | tf_op jit(solution)/shard_map/squeeze | solution.py:611
  63.9 0.7 %copy.10 = f32[3,16,1024]{2,1,0:T(8,128)} copy(f32[3,16,1024]{2,1,0:T(8,128)S(1)} %get-tuple-element.11) | data formatting | bytes 393216

commit v6 on v5

--- a/solution.py
+++ b/solution.py
@@ -372,6 +372,13 @@
 
     arrivals(A2A2, got2, quarter, BLOCK, use2, last2)
 
+    forward2 = remote(lens2, lens2, FWD2, fq + 1 - 2 * core, s)
+
+    @pl.when(mine)
+    def _():
+        wait_on(rs.at[LENS2], lens2.at[pl.ds(0, ROWS * (SHARDS - 1))])
+        forward2.start()
+
     def solve3(i, carry):
         n = lax.rem(k // 8 + i, 4)
         new = x_solve(0, xb[0], xb[1], n)
@@ -406,13 +413,6 @@
         return value
 
     sum_send(part0, sum0, SUM0)
-
-    forward2 = remote(lens2, lens2, FWD2, fq + 1 - 2 * core, s)
-
-    @pl.when(mine)
-    def _():
-        wait_on(rs.at[LENS2], lens2.at[pl.ds(0, ROWS * (SHARDS - 1))])
-        forward2.start()
 
     @pl.when(jnp.logical_not(mine))
     def _():

time: 64.6 us -> 63.6 us (0.985)
  Pallas kernels: 62.5 us -> 61.5 us
    pallas_call x1, Pallas kernels: 62.5 us -> 61.5 us  [on_device(): pl.pallas_call(kernel, out_shape=(vmem((2,) + source_field.shape, BF16),...]
where the time goes in v6:
time: 63.6 us; the launch traced here: 63.5 us
  Pallas kernels  61.5 us (97%)
  local copies, waits for them, and re-layouts  1.39 us (2%)
  between operations  0.64 us (1%)
    pallas_call x1, Pallas kernels, on_device(): pl.pallas_call(kernel, out_shape=(vmem((2,) + source_field.shape, BF16),...  61.5 us

profile of v6, /device:TPU:1, one launch (start us, length us, event | category | flops | bytes accessed | tf_op | source)
XLA Modules:
  0.0 63.5 jit_solution(6836174256028918454)
XLA Ops:
  0.6 61.5 %shard_map.85 = (bf16[2,2,2,16,1024]{4,3,2,1,0:T(8,128)(2,1)S(1)}, f32[3,16,1024]{2,1,0:T(8,128)S(1)}) custom-call(bf16[2,2,16,1024]{3,2,1,0:T(8,128)(2,1)} %src.1, bf16[2,2,16,1024]{3,2,1,0:T(8,128)(2,1)} %rcv.1, bf16[2,2,1024,1024]{3,2,1,0:T(8,128)(2,1)} %minv.1, f32[3,16,1024]{2,1,0:T(8,128)} %lens.1, f32[2]{0:T(128)} %om_hbm.1, f32[2]{0:T(128)} %wt_hbm.1), custom_call_target="tpu_custom_call" | custom-call | tf_op jit(solution)/shard_map/pallas_call | solution.py:579
  62.1 0.7 %slice_bitcast_fusion = (bf16[2,2,16,1024]{3,2,1,0:T(8,128)(2,1)}, bf16[2,2,16,1024]{3,2,1,0:T(8,128)(2,1)}) fusion(bf16[2,2,2,16,1024]{4,3,2,1,0:T(8,128)(2,1)S(1)} %get-tuple-element.5), kind=kLoop, calls=%fused_computation | loop fusion | bytes 524288 | tf_op jit(solution)/shard_map/squeeze | solution.py:611
  62.8 0.7 %copy.10 = f32[3,16,1024]{2,1,0:T(8,128)} copy(f32[3,16,1024]{2,1,0:T(8,128)S(1)} %get-tuple-element.11) | data formatting | bytes 393216
